TPU v7x, 256 devices: a whole 4x4x8 slice. The times are simulated.
256 devices in a mesh: sample: 16 (over y, x), space: 16 (over z, core).
Axes of the slice: x: 4, y: 4, z: 8, core: 2. Of those that a mesh axis runs over, the one named last changes fastest.
Arguments:
- slabs: bfloat16 [16, 64, 32, 3072], P('sample', 'space'), may hold values from -6 to 6
- weight: bfloat16 [3, 3, 3, 96, 192], replicated, may hold values from -0.125 to 0.125
- cotangent: bfloat16 [16, 32, 16, 3072], P('sample', 'space'), may hold values from -6 to 6
Outputs:
- activation: bfloat16 [16, 32, 16, 3072], P('sample', 'space')
- input_grad: bfloat16 [16, 64, 32, 3072], P('sample', 'space')
- weight_grad: float32 [3, 3, 3, 96, 192], P(None, None, None, None, 'space')
All inputs are finite; a program needn't handle non-finite values.
Results may differ from a plain program's by a relative error of at most 0.007.
Values may be sent and summed in bfloat16 or wider, within the bound.
A program may use at most 64 MiB of HBM per device.

v0:
```python
import jax
import jax.numpy as jnp
from jax import lax
from jax.sharding import PartitionSpec as P

CIN = 96
COUT = 192
DEPTH = 64
H = 32
W = 32
DOUT = 32
HOUT = 16
WOUT = 16


def from_behind(block, axis, distance):
    devices = range(lax.axis_size(axis))
    route = [(i - distance, i) for i in devices if i - distance in devices]
    return lax.ppermute(block, axis, route)


def parity_view(padded):
    count, depth_two, rows_two, cols_two, chans = padded.shape
    return padded.reshape(count, depth_two // 2, 2, rows_two // 2, 2, cols_two // 2, 2, chans)


def window_rows(parity, depth_off, row_off, col_off, out_d, out_h, out_w):
    piece = parity[
        :,
        depth_off // 2 : depth_off // 2 + out_d,
        depth_off % 2,
        row_off // 2 : row_off // 2 + out_h,
        row_off % 2,
        col_off // 2 : col_off // 2 + out_w,
        col_off % 2,
        :,
    ]
    return piece.reshape(-1, parity.shape[-1])


def conv_forward(padded, weight):
    count = padded.shape[0]
    out_d, out_h, out_w = (
        padded.shape[1] // 2 - 1,
        padded.shape[2] // 2 - 1,
        padded.shape[3] // 2 - 1,
    )
    parity = parity_view(padded)
    total = jnp.zeros((count * out_d * out_h * out_w, weight.shape[4]), jnp.float32)
    for depth_off in range(3):
        for row_off in range(3):
            for col_off in range(3):
                rows = window_rows(parity, depth_off, row_off, col_off, out_d, out_h, out_w)
                total = total + jnp.dot(
                    rows, weight[depth_off, row_off, col_off], preferred_element_type=jnp.float32
                )
    return total.reshape(count, out_d, out_h, out_w, weight.shape[4])


def kernel_terms(padded, grad_rows):
    out_d, out_h, out_w = (
        padded.shape[1] // 2 - 1,
        padded.shape[2] // 2 - 1,
        padded.shape[3] // 2 - 1,
    )
    parity = parity_view(padded)
    collected = []
    for depth_off in range(3):
        for row_off in range(3):
            for col_off in range(3):
                rows = window_rows(parity, depth_off, row_off, col_off, out_d, out_h, out_w)
                collected.append(
                    lax.dot_general(
                        rows,
                        grad_rows,
                        (((0,), (0,)), ((), ())),
                        preferred_element_type=jnp.float32,
                    )
                )
    return jnp.stack(collected).reshape(3, 3, 3, padded.shape[-1], grad_rows.shape[-1])


def padded_input_grad(grad_rows, weight, count, out_d, out_h, out_w):
    chans = weight.shape[3]
    buffers = {}
    for depth_off in range(3):
        for row_off in range(3):
            for col_off in range(3):
                term = jnp.dot(
                    grad_rows,
                    weight[depth_off, row_off, col_off].T,
                    preferred_element_type=jnp.float32,
                )
                term = term.reshape(count, out_d, out_h, out_w, chans)
                term = jnp.pad(
                    term,
                    (
                        (0, 0),
                        (depth_off // 2, 1 - depth_off // 2),
                        (row_off // 2, 1 - row_off // 2),
                        (col_off // 2, 1 - col_off // 2),
                        (0, 0),
                    ),
                )
                key_par = (depth_off % 2, row_off % 2, col_off % 2)
                if key_par in buffers:
                    buffers[key_par] = buffers[key_par] + term
                else:
                    buffers[key_par] = term
    ordered = [buffers[pd, ph, pw] for pd in range(2) for ph in range(2) for pw in range(2)]
    stacked = jnp.stack(ordered).reshape(2, 2, 2, count, out_d + 1, out_h + 1, out_w + 1, chans)
    stacked = jnp.transpose(stacked, (3, 4, 0, 5, 1, 6, 2, 7))
    return stacked.reshape(count, 2 * (out_d + 1), 2 * (out_h + 1), 2 * (out_w + 1), chans)


def derivative(preact):
    sigmoid_val = jax.nn.sigmoid(preact)
    return sigmoid_val * (1.0 + preact * (1.0 - sigmoid_val))


def per_device(slabs, weight, cotangent):
    group_size, depth_dev = (slabs.shape[0], slabs.shape[1])
    bands = lax.axis_size("space") // group_size
    band_rows = H // bands
    out_rows = band_rows // 2
    out_dev = depth_dev // 2
    cells = (
        slabs.reshape(group_size, depth_dev, bands, band_rows, W * CIN)
        .transpose(0, 2, 1, 3, 4)
        .reshape(group_size * bands, depth_dev, band_rows, W * CIN)
    )
    cot_cells = (
        cotangent.reshape(group_size, out_dev, bands, out_rows, WOUT * COUT)
        .transpose(0, 2, 1, 3, 4)
        .reshape(group_size * bands, out_dev, out_rows, WOUT * COUT)
    )
    whole_cells, whole_cot = (
        lax.all_to_all(cells, "space", split_axis=0, concat_axis=1, tiled=True),
        lax.all_to_all(cot_cells, "space", split_axis=0, concat_axis=1, tiled=True),
    )
    band_index = lax.axis_index("space") % bands
    inside = band_index != 0
    above = from_behind(whole_cells[:, :, band_rows - 1 :], "space", 1)
    above = jnp.where(inside, above, jnp.zeros_like(above))
    field = jnp.concatenate([above, whole_cells], axis=2).reshape(1, DEPTH, band_rows + 1, W, CIN)
    padded = jnp.pad(field, ((0, 0), (1, 1), (0, 1), (1, 1), (0, 0)))
    preact = conv_forward(padded, weight)
    result = jax.nn.silu(preact).astype(jnp.bfloat16)
    grad_pre = (whole_cot.reshape(preact.shape).astype(jnp.float32) * derivative(preact)).astype(
        jnp.bfloat16
    )
    grad_rows = grad_pre.reshape(-1, COUT)
    grad_pad = padded_input_grad(grad_rows, weight, 1, DOUT, out_rows, WOUT)
    grad_full = grad_pad[:, 1 : DEPTH + 1, :, 1 : W + 1].reshape(1, DEPTH, band_rows + 2, W * CIN)
    top_grad = grad_full[:, :, :1]
    top_grad = jnp.where(inside, top_grad, jnp.zeros_like(top_grad))
    below_grad = from_behind(top_grad.astype(jnp.bfloat16), "space", -1).astype(top_grad.dtype)
    grad_own = grad_full[:, :, 1 : band_rows + 1]
    grad_own = jnp.concatenate(
        [grad_own[:, :, : band_rows - 1], grad_own[:, :, band_rows - 1 :] + below_grad], axis=2
    )
    grad_in = grad_own.astype(jnp.bfloat16)
    partial_w = kernel_terms(padded, grad_rows)
    back_act, back_grad = (
        lax.all_to_all(
            result.reshape(1, DOUT, out_rows, WOUT * COUT),
            "space",
            split_axis=1,
            concat_axis=0,
            tiled=True,
        ),
        lax.all_to_all(grad_in, "space", split_axis=1, concat_axis=0, tiled=True),
    )
    activation = (
        back_act.reshape(group_size, bands, out_dev, out_rows, WOUT * COUT)
        .transpose(0, 2, 1, 3, 4)
        .reshape(group_size, out_dev, HOUT, WOUT * COUT)
    )
    input_grad = (
        back_grad.reshape(group_size, bands, depth_dev, band_rows, W * CIN)
        .transpose(0, 2, 1, 3, 4)
        .reshape(group_size, depth_dev, H, W * CIN)
    )
    batch_total = group_size * lax.axis_size("sample")
    summed = lax.psum(partial_w, "sample")
    gradient = lax.psum_scatter(summed, "space", scatter_dimension=4, tiled=True)
    return (activation, input_grad, gradient / batch_total)


def solution(mesh):
    placed = (P("sample", "space", None, None), P(), P("sample", "space", None, None))
    return jax.shard_map(
        per_device,
        mesh=mesh,
        in_specs=placed,
        out_specs=(
            P("sample", "space", None, None),
            P("sample", "space", None, None),
            P(None, None, None, None, "space"),
        ),
        check_vma=False,
    )
```

profile of v0, /device:TPU:2, one launch (start us, length us, event | category | flops | bytes accessed | tf_op | source)
XLA Modules:
  0.0 354.3 jit_solution(13199138809620854574)
XLA Ops:
  7.2 2.2 reshape.287
  10.1 30.9 %all_to_all.45 = bf16[16,4,2,3072]{3,2,1,0:T(2,128)(2,1)S(1)} all-to-all(bf16[16,4,2,3072]{3,2,1,0:T(2,128)(2,1)S(1)} %bitcast.587), channel_id=1, replica_groups=mesh['sample'=16,'space'=16] {'space'}, dimensions={0} | all-to-all | bytes 1572864 | tf_op jit(solution)/shard_map/all_to_all | solution.py:138
  42.0 2.9 collective-permute-start
  45.7 3.6 %all-to-all-start.2 = ((bf16[16,2,1,3072]{3,1,2,0:T(2,128)(2,1)}), bf16[16,2,1,3072]{3,1,2,0:T(2,128)(2,1)S(1)}, u32[]{:S(2)}, u32[]{:S(2)}) async-start(bf16[16,2,1,3072]{3,1,2,0:T(2,128)(2,1)} %bitcast.552), calls=%async_computation.2 | async-start | bytes 393216 | tf_op jit(solution)/shard_map/all_to_all | solution.py:139
  49.4 9.9 %all-to-all-done.2 = bf16[16,2,1,3072]{3,1,2,0:T(2,128)(2,1)S(1)} async-done(((bf16[16,2,1,3072]{3,1,2,0:T(2,128)(2,1)}), bf16[16,2,1,3072]{3,1,2,0:T(2,128)(2,1)S(1)}, u32[]{:S(2)}, u32[]{:S(2)}) %all-to-all-start.2) | async-done | bytes 196640 | tf_op jit(solution)/shard_map/all_to_all | solution.py:139
  62.2 1.1 copy.120
  63.3 1.1 pad.93.clone
  64.5 1.8 fusion.140
  66.3 4.2 %fusion.139 = (bf16[1,32,1,1,1,16,1,96]{7,4,3,6,5,2,1,0:T(2,128)(2,1)S(1)}, bf16[1,32,1,1,1,16,1,96]{7,4,3,6,5,2,1,0:T(2,128)(2,1)S(1)}, bf16[1,32,1,1,1,16,1,96...) fusion(bf16[1,33,2,2,2,17,2,96]{7,4,3,6,5,2,1,0:T(2,128)(2,1)S(, ...), kind=kLoop, calls=%fused_computation.239 | loop fusion | bytes 3735552 | tf_op jit(solution)/shard_map/slice | solution.py:28
  71.3 1.1 copy-done
  79.2 1.1 multiply_convert_fusion
  112.6 1.6 copy-done.2
  114.2 3.5 copy.87
  121.9 3.5 %copy.83 = f32[2,2,2,1,33,2,17,96]{7,1,5,2,6,0,4,3:T(2,128)S(1)} copy(f32[2,2,2,1,33,2,17,96]{7,6,4,5,2,1,0,3:T(8,128)S(1)} %bitcast.584) | data formatting | bytes 6893568 | tf_op jit(solution)/shard_map/reshape | solution.py:111
  126.0 2.6 copy.84
  128.6 4.4 %reshape.297 = f32[1,64,4,3072]{3,1,2,0:T(8,128)S(1)} reshape(f32[1,64,4,32,96]{4,3,1,2,0:T(8,128)} %copy.84) | data formatting | bytes 6291456 | tf_op jit(solution)/shard_map/reshape | solution.py:154
  134.1 1.3 collective-permute-start.1
  136.4 1.3 reshape.290
  138.6 2.5 reduce.2
  141.0 1.7 reshape.332
  142.7 6.2 %all-to-all-start.1 = ((bf16[16,2,3072]{2,1,0:T(2,128)(2,1)}), bf16[16,2,3072]{2,1,0:T(2,128)(2,1)}, u32[]{:S(2)}, u32[]{:S(2)}) async-start(bf16[16,2,3072]{2,1,0:T(2,128)(2,1)} %reshape.332), calls=%async_computation.1 | async-start | bytes 393216 | tf_op jit(solution)/shard_map/all_to_all | solution.py:165
  148.9 1.1 fusion.28
  150.1 1.7 copy.85
  151.8 6.9 %all-to-all-done.1 = bf16[16,2,3072]{2,1,0:T(2,128)(2,1)} async-done(((bf16[16,2,3072]{2,1,0:T(2,128)(2,1)}), bf16[16,2,3072]{2,1,0:T(2,128)(2,1)}, u32[]{:S(2)}, u32[]{:S(2)}) %all-to-all-start.1) | async-done | bytes 196640 | tf_op jit(solution)/shard_map/all_to_all | solution.py:165
  158.7 4.5 %all-to-all-start.3 = ((bf16[1,64,2,3072]{3,2,0,1:T(2,128)(2,1)}), bf16[1,64,2,3072]{3,2,0,1:T(2,128)(2,1)S(1)}, u32[]{:S(2)}, u32[]{:S(2)}) async-start(bf16[1,64,2,3072]{3,2,0,1:T(2,128)(2,1)} %copy.85), calls=%async_computation.3 | async-start | bytes 1572864 | tf_op jit(solution)/shard_map/all_to_all | solution.py:172
  164.4 1.8 reshape.333
  166.3 80.0 %all-reduce.34.cloned.1.call-done = f32[3,3,3,96,192]{3,4,2,1,0:T(8,128)} async-done(((f32[3,3,3,96,192]{3,4,2,1,0:T(8,128)}), f32[3,3,3,96,192]{3,4,2,1,0:T(8,128)}) %all-reduce.34.cloned.1.call-update) | async-done | bytes 1990672
  246.3 1.7 constant_dynamic-slice_fusion
  248.0 1.1 bitcast_reduce_fusion
  249.9 94.4 %all-reduce.32.cloned.1.call-done = f32[3,3,3,96,12]{3,4,2,1,0:T(8,128)} async-done(((f32[3,3,3,96,12]{3,4,2,1,0:T(8,128)}), f32[3,3,3,96,12]{3,4,2,1,0:T(8,128)}) %all-reduce.32.cloned.1.call-update) | async-done | bytes 124432 | tf_op jit(solution)/shard_map/psum | solution.py:185
  344.3 1.6 broadcast_multiply_fusion
  346.3 1.1 copy.89
  (264 shorter events, 53.9 us)
Async XLA Ops:
  10.1 34.8 %copy-start.59 = (bf16[1,2,16,3072]{3,2,1,0:T(8,128)(2,1)S(1)}, bf16[1,2,16,3072]{3,2,1,0:T(8,128)(2,1)}, u32[]{:S(2)}) copy-start(bf16[1,2,16,3072]{3,2,1,0:T(8,128)(2,1)} %param.5) | copy-start | bytes 589828
  42.0 19.4 %collective-permute-start = (bf16[1,64,1,3072]{3,1,2,0:T(8,128)(2,1)S(1)}, bf16[1,64,1,3072]{3,1,2,0:T(8,128)(2,1)S(1)}, u32[]{:S(2)}, u32[]{:S(2)}) collective-permute-start(bf16[1,64,1,3072]{3,1,2,0:T(8,128)(2,1)S(1)} %copy.75), channel_id=1, source_target_pairs={{0,1},{1,2},{2,3},{3,4},{4,5},{5,6},{6,7},{7,8},{8,9},{9,10},{10,1... | collective-permute-start | bytes 1179656 | tf_op jit(solution)/shard_map/ppermute | solution.py:19
  45.7 13.6 %all-to-all-start.2 = ((bf16[16,2,1,3072]{3,1,2,0:T(2,128)(2,1)}), bf16[16,2,1,3072]{3,1,2,0:T(2,128)(2,1)S(1)}, u32[]{:S(2)}, u32[]{:S(2)}) async-start(bf16[16,2,1,3072]{3,1,2,0:T(2,128)(2,1)} %bitcast.552), calls=%async_computation.2 | async-start | bytes 393216 | tf_op jit(solution)/shard_map/all_to_all | solution.py:139
  49.4 196.9 %all-reduce.34.cloned.1.call-start = ((), (), s32[]{:S(2)}) async-start(), calls=%async_computation.5 | async-start | bytes 5308416
  70.6 3.1 copy-start.18
  70.7 3.3 copy-start.14
  70.7 3.5 %copy-start.16 = (bf16[1,32,1,1,1,16,1,96]{7,5,3,6,4,2,1,0:T(8,128)(2,1)}, bf16[1,32,1,1,1,16,1,96]{7,5,3,6,4,2,1,0:T(8,128)(2,1)S(1)}, u32[]{:S(2)}) copy-start(bf16[1,32,1,1,1,16,1,96]{7,5,3,6,4,2,1,0:T(8,128)(2,1)S(1)} %copy.99) | copy-start | bytes 294916
  70.8 3.8 %copy-start.12 = (bf16[1,32,1,1,1,16,1,96]{7,5,3,6,4,2,1,0:T(8,128)(2,1)}, bf16[1,32,1,1,1,16,1,96]{7,5,3,6,4,2,1,0:T(8,128)(2,1)S(1)}, u32[]{:S(2)}) copy-start(bf16[1,32,1,1,1,16,1,96]{7,5,3,6,4,2,1,0:T(8,128)(2,1)S(1)} %copy.100) | copy-start | bytes 294916
  70.8 4.0 %copy-start.10 = (bf16[1,32,1,1,1,16,1,96]{7,5,3,6,4,2,1,0:T(8,128)(2,1)}, bf16[1,32,1,1,1,16,1,96]{7,5,3,6,4,2,1,0:T(8,128)(2,1)S(1)}, u32[]{:S(2)}) copy-start(bf16[1,32,1,1,1,16,1,96]{7,5,3,6,4,2,1,0:T(8,128)(2,1)S(1)} %copy.101) | copy-start | bytes 294916
  70.8 4.2 %copy-start.8 = (bf16[1,32,1,1,1,16,1,96]{7,5,3,6,4,2,1,0:T(8,128)(2,1)}, bf16[1,32,1,1,1,16,1,96]{7,5,3,6,4,2,1,0:T(8,128)(2,1)S(1)}, u32[]{:S(2)}) copy-start(bf16[1,32,1,1,1,16,1,96]{7,5,3,6,4,2,1,0:T(8,128)(2,1)S(1)} %copy.102) | copy-start | bytes 294916
  70.9 4.5 %copy-start.6 = (bf16[1,32,1,1,1,16,1,96]{7,5,3,6,4,2,1,0:T(8,128)(2,1)}, bf16[1,32,1,1,1,16,1,96]{7,5,3,6,4,2,1,0:T(8,128)(2,1)S(1)}, u32[]{:S(2)}) copy-start(bf16[1,32,1,1,1,16,1,96]{7,5,3,6,4,2,1,0:T(8,128)(2,1)S(1)} %copy.103) | copy-start | bytes 294916
  70.9 4.7 %copy-start.4 = (bf16[1,32,1,1,1,16,1,96]{7,5,3,6,4,2,1,0:T(8,128)(2,1)}, bf16[1,32,1,1,1,16,1,96]{7,5,3,6,4,2,1,0:T(8,128)(2,1)S(1)}, u32[]{:S(2)}) copy-start(bf16[1,32,1,1,1,16,1,96]{7,5,3,6,4,2,1,0:T(8,128)(2,1)S(1)} %copy.104) | copy-start | bytes 294916
  71.3 7.9 %copy-start.55 = (bf16[1,32,1,1,1,16,1,96]{7,5,3,6,4,2,1,0:T(8,128)(2,1)}, bf16[1,32,1,1,1,16,1,96]{7,5,3,6,4,2,1,0:T(8,128)(2,1)S(1)}, u32[]{:S(2)}) copy-start(bf16[1,32,1,1,1,16,1,96]{7,5,3,6,4,2,1,0:T(8,128)(2,1)S(1)} %copy.118) | copy-start | bytes 294916
  99.0 7.5 %copy-start.1 = (f32[27,96,192]{2,1,0:T(8,128)S(1)}, f32[27,96,192]{2,1,0:T(8,128)}, u32[]{:S(2)}) copy-start(f32[27,96,192]{2,1,0:T(8,128)} %fusion.26) | copy-start | bytes 5971972
  99.0 7.5 %copy-start.27 = (bf16[1,32,1,1,1,16,1,96]{7,5,3,6,4,2,1,0:T(8,128)(2,1)S(1)}, bf16[1,32,1,1,1,16,1,96]{7,5,3,6,4,2,1,0:T(8,128)(2,1)}, u32[]{:S(2)}) copy-start(bf16[1,32,1,1,1,16,1,96]{7,5,3,6,4,2,1,0:T(8,128)(2,1)} %copy-done.26) | copy-start | bytes 294916
  100.0 6.8 %copy-start.25 = (bf16[1,32,1,1,1,16,1,96]{7,5,3,6,4,2,1,0:T(8,128)(2,1)S(1)}, bf16[1,32,1,1,1,16,1,96]{7,5,3,6,4,2,1,0:T(8,128)(2,1)}, u32[]{:S(2)}) copy-start(bf16[1,32,1,1,1,16,1,96]{7,5,3,6,4,2,1,0:T(8,128)(2,1)} %copy-done.24) | copy-start | bytes 294916
  100.0 7.0 %copy-start.23 = (bf16[1,32,1,1,1,16,1,96]{7,5,3,6,4,2,1,0:T(8,128)(2,1)S(1)}, bf16[1,32,1,1,1,16,1,96]{7,5,3,6,4,2,1,0:T(8,128)(2,1)}, u32[]{:S(2)}) copy-start(bf16[1,32,1,1,1,16,1,96]{7,5,3,6,4,2,1,0:T(8,128)(2,1)} %copy-done.22) | copy-start | bytes 294916
  100.9 6.3 %copy-start.21 = (bf16[1,32,1,1,1,16,1,96]{7,5,3,6,4,2,1,0:T(8,128)(2,1)S(1)}, bf16[1,32,1,1,1,16,1,96]{7,5,3,6,4,2,1,0:T(8,128)(2,1)}, u32[]{:S(2)}) copy-start(bf16[1,32,1,1,1,16,1,96]{7,5,3,6,4,2,1,0:T(8,128)(2,1)} %copy-done.20) | copy-start | bytes 294916
  101.8 5.6 %copy-start.19 = (bf16[1,32,1,1,1,16,1,96]{7,5,3,6,4,2,1,0:T(8,128)(2,1)S(1)}, bf16[1,32,1,1,1,16,1,96]{7,5,3,6,4,2,1,0:T(8,128)(2,1)}, u32[]{:S(2)}) copy-start(bf16[1,32,1,1,1,16,1,96]{7,5,3,6,4,2,1,0:T(8,128)(2,1)} %copy-done.18) | copy-start | bytes 294916
  102.8 4.9 %copy-start.15 = (bf16[1,32,1,1,1,16,1,96]{7,5,3,6,4,2,1,0:T(8,128)(2,1)S(1)}, bf16[1,32,1,1,1,16,1,96]{7,5,3,6,4,2,1,0:T(8,128)(2,1)}, u32[]{:S(2)}) copy-start(bf16[1,32,1,1,1,16,1,96]{7,5,3,6,4,2,1,0:T(8,128)(2,1)} %copy-done.14) | copy-start | bytes 294916
  102.8 5.2 %copy-start.17 = (bf16[1,32,1,1,1,16,1,96]{7,5,3,6,4,2,1,0:T(8,128)(2,1)S(1)}, bf16[1,32,1,1,1,16,1,96]{7,5,3,6,4,2,1,0:T(8,128)(2,1)}, u32[]{:S(2)}) copy-start(bf16[1,32,1,1,1,16,1,96]{7,5,3,6,4,2,1,0:T(8,128)(2,1)} %copy-done.16) | copy-start | bytes 294916
  103.7 4.5 %copy-start.13 = (bf16[1,32,1,1,1,16,1,96]{7,5,3,6,4,2,1,0:T(8,128)(2,1)S(1)}, bf16[1,32,1,1,1,16,1,96]{7,5,3,6,4,2,1,0:T(8,128)(2,1)}, u32[]{:S(2)}) copy-start(bf16[1,32,1,1,1,16,1,96]{7,5,3,6,4,2,1,0:T(8,128)(2,1)} %copy-done.12) | copy-start | bytes 294916
  104.6 3.8 %copy-start.11 = (bf16[1,32,1,1,1,16,1,96]{7,5,3,6,4,2,1,0:T(8,128)(2,1)S(1)}, bf16[1,32,1,1,1,16,1,96]{7,5,3,6,4,2,1,0:T(8,128)(2,1)}, u32[]{:S(2)}) copy-start(bf16[1,32,1,1,1,16,1,96]{7,5,3,6,4,2,1,0:T(8,128)(2,1)} %copy-done.10) | copy-start | bytes 294916
  105.6 3.1 copy-start.9
  105.6 3.3 copy-start.7
  128.6 6.7 %copy-start.57 = (f32[512,192]{0,1:T(8,128)S(1)}, f32[512,192]{0,1:T(8,128)}, u32[]{:S(2)}) copy-start(f32[512,192]{0,1:T(8,128)} %get-tuple-element.45) | copy-start | bytes 1179652
  134.1 14.9 %collective-permute-start.1 = (bf16[1,64,1,3072]{3,1,2,0:T(8,128)(2,1)}, bf16[1,64,1,3072]{3,1,2,0:T(8,128)(2,1)}, u32[]{:S(2)}, u32[]{:S(2)}) collective-permute-start(bf16[1,64,1,3072]{3,1,2,0:T(8,128)(2,1)} %get-tuple-element.16), channel_id=1, source_target_pairs={{1,0},{2,1},{3,2},{4,3},{5,4},{6,5},{7,6},{8,7},{9,8},{10,9},{11,1... | collective-permute-start | bytes 1179656 | tf_op jit(solution)/shard_map/ppermute | solution.py:19
  141.0 9.0 %copy-start.3 = (bf16[1,64,1,3072]{3,1,2,0:T(8,128)(2,1)S(1)}, bf16[1,64,1,3072]{3,1,2,0:T(8,128)(2,1)}, u32[]{:S(2)}) copy-start(bf16[1,64,1,3072]{3,1,2,0:T(8,128)(2,1)} %get-tuple-element.15) | copy-start | bytes 1179652
  142.7 15.9 %all-to-all-start.1 = ((bf16[16,2,3072]{2,1,0:T(2,128)(2,1)}), bf16[16,2,3072]{2,1,0:T(2,128)(2,1)}, u32[]{:S(2)}, u32[]{:S(2)}) async-start(bf16[16,2,3072]{2,1,0:T(2,128)(2,1)} %reshape.332), calls=%async_computation.1 | async-start | bytes 393216 | tf_op jit(solution)/shard_map/all_to_all | solution.py:165
  150.0 13.2 %copy-start.60 = (u32[256]{0:T(256)S(1)}, u32[256]{0:T(256)}, u32[]{:S(2)}) copy-start(u32[256]{0:T(256)} %constant.91) | copy-start | bytes 3076
  158.7 187.3 %all-to-all-start.3 = ((bf16[1,64,2,3072]{3,2,0,1:T(2,128)(2,1)}), bf16[1,64,2,3072]{3,2,0,1:T(2,128)(2,1)S(1)}, u32[]{:S(2)}, u32[]{:S(2)}) async-start(bf16[1,64,2,3072]{3,2,0,1:T(2,128)(2,1)} %copy.85), calls=%async_computation.3 | async-start | bytes 1572864 | tf_op jit(solution)/shard_map/all_to_all | solution.py:172
  163.1 181.2 %all-reduce.32.cloned.1.call-start = ((), (), s32[]{:S(2)}) async-start(), calls=%async_computation.4 | async-start | bytes 442368 | tf_op jit(solution)/shard_map/psum | solution.py:185
  (36 other events, 53.3 us)
Sparse Core Ops, SparseCore 0:
  117.8 128.3 all-reduce.33
  250.4 93.8 all-reduce.31
where the time goes:
time: 356 us; the launch traced here: 354 us
  waiting for transfers between devices  191 us (54%)
  local copies, waits for them, and re-layouts  50.7 us (14%)
  matrix products  39.3 us (11%)
  blocking collectives  30.9 us (9%)
  starting transfers between devices  18.5 us (5%)
  between operations  16.2 us (5%)
  other arithmetic  7.45 us (2%)
    psum x1, waiting for transfers between devices, per_device(): summed = lax.psum(partial_w, 'sample')  94.4 us
    unnamed x3, waiting for transfers between devices  80 us
    all_to_all x1, blocking collectives, per_device(): lax.all_to_all(cells, 'space', split_axis=0, concat_axis=1, tiled=True)  30.9 us
    dot_general x27, matrix products, padded_input_grad(): jnp.dot(grad_rows, weight[depth_off, row_off, col_off].T, preferred_eleme...  25.2 us
    unnamed x158, local copies, waits for them, and re-layouts  16.8 us
    all_to_all x1, waiting for transfers between devices, per_device(): lax.all_to_all(cot_cells, 'space', split_axis=0, concat_axis=1, tiled=True)  9.89 us
    dot_general x27, matrix products, conv_forward(): jnp.dot(rows, weight[depth_off, row_off, col_off], preferred_element_type...  7.54 us
  transfers between devices with their start and end apart: 7, of which 4 were waited for; matrix products, arithmetic and copies ran while one was open for 9% of the time, Pallas kernels for 0%

commit v1 on v0

--- a/solution.py
+++ b/solution.py
@@ -119,72 +119,28 @@
 
 
 def per_device(slabs, weight, cotangent):
-    group_size, depth_dev = (slabs.shape[0], slabs.shape[1])
-    bands = lax.axis_size("space") // group_size
-    band_rows = H // bands
-    out_rows = band_rows // 2
+    depth_dev = slabs.shape[1]
     out_dev = depth_dev // 2
-    cells = (
-        slabs.reshape(group_size, depth_dev, bands, band_rows, W * CIN)
-        .transpose(0, 2, 1, 3, 4)
-        .reshape(group_size * bands, depth_dev, band_rows, W * CIN)
-    )
-    cot_cells = (
-        cotangent.reshape(group_size, out_dev, bands, out_rows, WOUT * COUT)
-        .transpose(0, 2, 1, 3, 4)
-        .reshape(group_size * bands, out_dev, out_rows, WOUT * COUT)
-    )
-    whole_cells, whole_cot = (
-        lax.all_to_all(cells, "space", split_axis=0, concat_axis=1, tiled=True),
-        lax.all_to_all(cot_cells, "space", split_axis=0, concat_axis=1, tiled=True),
-    )
-    band_index = lax.axis_index("space") % bands
-    inside = band_index != 0
-    above = from_behind(whole_cells[:, :, band_rows - 1 :], "space", 1)
-    above = jnp.where(inside, above, jnp.zeros_like(above))
-    field = jnp.concatenate([above, whole_cells], axis=2).reshape(1, DEPTH, band_rows + 1, W, CIN)
-    padded = jnp.pad(field, ((0, 0), (1, 1), (0, 1), (1, 1), (0, 0)))
+    before = from_behind(slabs[:, depth_dev - 1 :], "space", 1)
+    field = jnp.concatenate([before, slabs], axis=1).reshape(1, depth_dev + 1, H, W, CIN)
+    padded = jnp.pad(field, ((0, 0), (0, 1), (1, 1), (1, 1), (0, 0)))
     preact = conv_forward(padded, weight)
     result = jax.nn.silu(preact).astype(jnp.bfloat16)
-    grad_pre = (whole_cot.reshape(preact.shape).astype(jnp.float32) * derivative(preact)).astype(
+    grad_pre = (cotangent.reshape(preact.shape).astype(jnp.float32) * derivative(preact)).astype(
         jnp.bfloat16
     )
-    grad_rows = grad_pre.reshape(-1, COUT)
-    grad_pad = padded_input_grad(grad_rows, weight, 1, DOUT, out_rows, WOUT)
-    grad_full = grad_pad[:, 1 : DEPTH + 1, :, 1 : W + 1].reshape(1, DEPTH, band_rows + 2, W * CIN)
-    top_grad = grad_full[:, :, :1]
-    top_grad = jnp.where(inside, top_grad, jnp.zeros_like(top_grad))
-    below_grad = from_behind(top_grad.astype(jnp.bfloat16), "space", -1).astype(top_grad.dtype)
-    grad_own = grad_full[:, :, 1 : band_rows + 1]
-    grad_own = jnp.concatenate(
-        [grad_own[:, :, : band_rows - 1], grad_own[:, :, band_rows - 1 :] + below_grad], axis=2
+    after = from_behind(grad_pre[:, :1], "space", -1)
+    partial_w = kernel_terms(padded, grad_pre.reshape(-1, COUT))
+    gradient = lax.psum_scatter(partial_w, "space", scatter_dimension=4, tiled=True)
+    gradient = lax.psum(gradient, "sample") / lax.axis_size("sample")
+    grad_ext = jnp.concatenate([grad_pre, after], axis=1).reshape(-1, COUT)
+    grad_pad = padded_input_grad(grad_ext, weight, 1, out_dev + 1, HOUT, WOUT)
+    grad_in = grad_pad[:, 1 : depth_dev + 1, 1 : H + 1, 1 : W + 1].astype(jnp.bfloat16)
+    return (
+        result.reshape(1, out_dev, HOUT, WOUT * COUT),
+        grad_in.reshape(1, depth_dev, H, W * CIN),
+        gradient,
     )
-    grad_in = grad_own.astype(jnp.bfloat16)
-    partial_w = kernel_terms(padded, grad_rows)
-    back_act, back_grad = (
-        lax.all_to_all(
-            result.reshape(1, DOUT, out_rows, WOUT * COUT),
-            "space",
-            split_axis=1,
-            concat_axis=0,
-            tiled=True,
-        ),
-        lax.all_to_all(grad_in, "space", split_axis=1, concat_axis=0, tiled=True),
-    )
-    activation = (
-        back_act.reshape(group_size, bands, out_dev, out_rows, WOUT * COUT)
-        .transpose(0, 2, 1, 3, 4)
-        .reshape(group_size, out_dev, HOUT, WOUT * COUT)
-    )
-    input_grad = (
-        back_grad.reshape(group_size, bands, depth_dev, band_rows, W * CIN)
-        .transpose(0, 2, 1, 3, 4)
-        .reshape(group_size, depth_dev, H, W * CIN)
-    )
-    batch_total = group_size * lax.axis_size("sample")
-    summed = lax.psum(partial_w, "sample")
-    gradient = lax.psum_scatter(summed, "space", scatter_dimension=4, tiled=True)
-    return (activation, input_grad, gradient / batch_total)
 
 
 def solution(mesh):

time: 356 us -> 285 us (0.80)
  blocking collectives: 30.9 us -> 0 us
  matrix products: 39.3 us -> 20 us
  starting transfers between devices: 18.5 us -> 3.29 us
  local copies, waits for them, and re-layouts: 50.7 us -> 37 us
  waiting for transfers between devices: 191 us -> 197 us
    all_to_all x1 -> x0, blocking collectives: 30.9 us -> none  [per_device(): lax.all_to_all(cells, 'space', split_axis=0, concat_axis=1, tiled=True)]
    unnamed x3, waiting for transfers between devices: 80 us -> 110 us
    dot_general x27, matrix products: 25.2 us -> 7.21 us  [padded_input_grad(): jnp.dot(grad_rows, weight[depth_off, row_off, col_off].T, preferred_eleme...]
    all_to_all x3 -> x0, waiting for transfers between devices: 16.8 us -> none  [the longest x1 9.89 us: per_device(): lax.all_to_all(cot_cells, 'space', split_axis=0, concat_axis=1, tiled=True)]
    all_to_all x3 -> x0, starting transfers between devices: 14.3 us -> none  [the longest x1 6.17 us: per_device(): lax.all_to_all(result.reshape(1, DOUT, out_rows, WOUT * COUT), 'space', s...]
    unnamed x158 -> x133, local copies, waits for them, and re-layouts: 16.8 us -> 5.92 us
    psum x1, waiting for transfers between devices: 94.4 us -> 87 us  [per_device(): gradient = lax.psum(gradient, 'sample') / lax.axis_size('sample')]
  transfers between devices with their start and end apart: 7 -> 4, of which waited for: 4 -> 2; matrix products, arithmetic and copies ran while one was open for 9% -> 13% of each run, Pallas kernels for 0% -> 0%
where the time goes in v1:
time: 285 us; the launch traced here: 283 us
  waiting for transfers between devices  197 us (69%)
  local copies, waits for them, and re-layouts  37 us (13%)
  matrix products  20 us (7%)
  between operations  16.4 us (6%)
  other arithmetic  9.36 us (3%)
  starting transfers between devices  3.29 us (1%)
    unnamed x3, waiting for transfers between devices  110 us
    psum x1, waiting for transfers between devices, per_device(): gradient = lax.psum(gradient, 'sample') / lax.axis_size('sample')  87 us
    dot_general x27, matrix products, padded_input_grad(): jnp.dot(grad_rows, weight[depth_off, row_off, col_off].T, preferred_eleme...  7.21 us
    dot_general x27, matrix products, conv_forward(): jnp.dot(rows, weight[depth_off, row_off, col_off], preferred_element_type...  6.86 us
    unnamed x7, other arithmetic  6.64 us
    unnamed x133, local copies, waits for them, and re-layouts  5.92 us
    slice x2, local copies, waits for them, and re-layouts, window_rows(): parity[:, depth_off // 2:depth_off // 2 + out_d, depth_off % 2, row_off /...  5.92 us
    dot_general x27, matrix products, kernel_terms(): lax.dot_general(rows, grad_rows, (((0,), (0,)), ((), ())), preferred_elem...  5.88 us
  transfers between devices with their start and end apart: 4, of which 2 were waited for; matrix products, arithmetic and copies ran while one was open for 13% of the time, Pallas kernels for 0%

profile of v1, /device:TPU:2, one launch (start us, length us, event | category | flops | bytes accessed | tf_op | source)
XLA Modules:
  0.0 283.2 jit_solution(13769606057288372673)
XLA Ops:
  7.2 1.0 slice.226
  8.2 1.8 collective-permute-start
  10.0 1.2 reshape.294
  11.2 2.0 reshape.293
  13.2 0.9 copy.24
  14.1 0.6 dynamic-slice
  15.5 1.3 reshape.284
  16.8 2.0 pad.94
  18.8 3.9 %reshape.285 = bf16[1,3,2,17,2,17,2,96]{7,6,5,4,3,2,1,0:T(2,128)(2,1)S(1)} reshape(bf16[1,6,34,34,96]{4,3,2,1,0:T(8,128)(2,1)} %pad.94) | data formatting | bytes 2663424 | tf_op jit(solution)/shard_map/reshape | solution.py:24
  22.7 1.6 fusion.150
  24.3 4.3 %fusion.149 = (bf16[1,2,1,16,1,16,1,96]{7,6,5,4,3,2,1,0:T(2,128)(2,1)S(1)}, bf16[1,2,1,16,1,16,1,96]{7,6,5,4,3,2,1,0:T(2,128)(2,1)S(1)}, bf16[1,2,1,16,1,16,1,96...) fusion(bf16[1,3,2,17,2,17,2,96]{7,6,5,4,3,2,1,0:T(2,128)(2,1)S(, ...), kind=kLoop, calls=%fused_computation.245 | loop fusion | bytes 3735552 | tf_op jit(solution)/shard_map/slice | solution.py:28
  29.7 1.4 copy-done
  38.9 0.8 multiply_convert_fusion.2
  39.9 0.7 slice.310
  40.6 1.5 collective-permute-start.1
  48.5 1.5 copy-done.1
  50.0 3.4 %copy.25 = f32[3,3,3,96,192]{3,4,2,1,0:T(8,128)} copy(f32[3,3,3,96,192]{4,3,2,1,0:T(8,128)} %bitcast.593) | data formatting | bytes 3981312 | tf_op jit(solution)/shard_map/reshape | solution.py:80
  55.7 1.2 bitcast_dynamic-update-slice_fusion.1
  58.0 0.9 fusion.29
  60.0 1.0 fusion.31
  62.6 0.8 fusion.33
  63.4 1.0 fusion.35
  64.9 0.9 fusion.37
  66.6 110.1 %all-reduce.34.cloned.1.call-done = f32[3,3,3,96,192]{3,4,2,1,0:T(8,128)} async-done(((f32[3,3,3,96,192]{3,4,2,1,0:T(8,128)}), f32[3,3,3,96,192]{3,4,2,1,0:T(8,128)}) %all-reduce.34.cloned.1.call-update) | async-done | bytes 1990672
  176.7 1.7 constant_dynamic-slice_fusion
  178.4 0.9 fusion.39
  179.3 0.8 bitcast_dynamic-update-slice_fusion
  180.1 4.5 %copy.22 = bf16[2,2,2,1,4,17,17,96]{7,0,4,2,6,1,5,3:T(2,128)(2,1)S(1)} copy(bf16[2,2,2,1,4,17,17,96]{7,6,5,4,2,1,0,3:T(8,128)(2,1)} %bitcast.118) | data formatting | bytes 3551232 | tf_op jit(solution)/shard_map/reshape | solution.py:111
  184.6 0.6 slice.311
  185.4 2.3 reshape.291
  187.7 87.0 %all-reduce.32.cloned.1.call-done = f32[3,3,3,96,12]{3,4,2,1,0:T(8,128)} async-done(((f32[3,3,3,96,12]{3,4,2,1,0:T(8,128)}), f32[3,3,3,96,12]{3,4,2,1,0:T(8,128)}) %all-reduce.32.cloned.1.call-update) | async-done | bytes 124432 | tf_op jit(solution)/shard_map/psum | solution.py:135
  274.7 1.6 broadcast_multiply_fusion
  (221 shorter events, 21.7 us)
Async XLA Ops:
  7.2 7.0 %copy-start.51 = (u32[256]{0:T(256)S(1)}, u32[256]{0:T(256)}, u32[]{:S(2)}) copy-start(u32[256]{0:T(256)} %constant.73) | copy-start | bytes 3076
  7.2 8.2 %copy-start.3 = (bf16[1,4,32,3072]{3,2,1,0:T(8,128)(2,1)S(1)}, bf16[1,4,32,3072]{3,2,1,0:T(8,128)(2,1)}, u32[]{:S(2)}) copy-start(bf16[1,4,32,3072]{3,2,1,0:T(8,128)(2,1)} %param.3) | copy-start | bytes 2359300
  7.2 169.5 %all-reduce.34.cloned.1.call-start = ((), (), s32[]{:S(2)}) async-start(), calls=%async_computation.1 | async-start | bytes 5308416
  8.2 7.1 %collective-permute-start = (bf16[1,1,32,3072]{3,2,1,0:T(8,128)(2,1)S(1)}, bf16[1,1,32,3072]{3,2,1,0:T(8,128)(2,1)S(1)}, u32[]{:S(2)}, u32[]{:S(2)}) collective-permute-start(bf16[1,1,32,3072]{3,2,1,0:T(8,128)(2,1)S(1)} %slice.226), channel_id=1, source_target_pairs={{0,1},{1,2},{2,3},{3,4},{4,5},{5,6},{6,7},{7,8},{8,9},{9,10},{10,1... | collective-permute-start | bytes 589832 | tf_op jit(solution)/shard_map/ppermute | solution.py:19
  28.9 3.5 %copy-start.38 = (bf16[1,2,1,16,1,16,1,96]{7,5,6,4,3,2,1,0:T(8,128)(2,1)}, bf16[1,2,1,16,1,16,1,96]{7,5,6,4,3,2,1,0:T(8,128)(2,1)S(1)}, u32[]{:S(2)}) copy-start(bf16[1,2,1,16,1,16,1,96]{7,5,6,4,3,2,1,0:T(8,128)(2,1)S(1)} %copy.60) | copy-start | bytes 294916
  28.9 3.8 %copy-start.34 = (bf16[1,2,1,16,1,16,1,96]{7,5,6,4,3,2,1,0:T(8,128)(2,1)}, bf16[1,2,1,16,1,16,1,96]{7,5,6,4,3,2,1,0:T(8,128)(2,1)S(1)}, u32[]{:S(2)}) copy-start(bf16[1,2,1,16,1,16,1,96]{7,5,6,4,3,2,1,0:T(8,128)(2,1)S(1)} %copy.61) | copy-start | bytes 294916
  28.9 4.0 %copy-start.36 = (bf16[1,2,1,16,1,16,1,96]{7,5,6,4,3,2,1,0:T(8,128)(2,1)}, bf16[1,2,1,16,1,16,1,96]{7,5,6,4,3,2,1,0:T(8,128)(2,1)S(1)}, u32[]{:S(2)}) copy-start(bf16[1,2,1,16,1,16,1,96]{7,5,6,4,3,2,1,0:T(8,128)(2,1)S(1)} %copy.62) | copy-start | bytes 294916
  29.0 4.2 %copy-start.32 = (bf16[1,2,1,16,1,16,1,96]{7,5,6,4,3,2,1,0:T(8,128)(2,1)}, bf16[1,2,1,16,1,16,1,96]{7,5,6,4,3,2,1,0:T(8,128)(2,1)S(1)}, u32[]{:S(2)}) copy-start(bf16[1,2,1,16,1,16,1,96]{7,5,6,4,3,2,1,0:T(8,128)(2,1)S(1)} %copy.63) | copy-start | bytes 294916
  29.0 4.5 %copy-start.30 = (bf16[1,2,1,16,1,16,1,96]{7,5,6,4,3,2,1,0:T(8,128)(2,1)}, bf16[1,2,1,16,1,16,1,96]{7,5,6,4,3,2,1,0:T(8,128)(2,1)S(1)}, u32[]{:S(2)}) copy-start(bf16[1,2,1,16,1,16,1,96]{7,5,6,4,3,2,1,0:T(8,128)(2,1)S(1)} %copy.64) | copy-start | bytes 294916
  29.1 4.7 %copy-start.28 = (bf16[1,2,1,16,1,16,1,96]{7,5,6,4,3,2,1,0:T(8,128)(2,1)}, bf16[1,2,1,16,1,16,1,96]{7,5,6,4,3,2,1,0:T(8,128)(2,1)S(1)}, u32[]{:S(2)}) copy-start(bf16[1,2,1,16,1,16,1,96]{7,5,6,4,3,2,1,0:T(8,128)(2,1)S(1)} %copy.65) | copy-start | bytes 294916
  29.1 4.9 %copy-start.26 = (bf16[1,2,1,16,1,16,1,96]{7,5,6,4,3,2,1,0:T(8,128)(2,1)}, bf16[1,2,1,16,1,16,1,96]{7,5,6,4,3,2,1,0:T(8,128)(2,1)S(1)}, u32[]{:S(2)}) copy-start(bf16[1,2,1,16,1,16,1,96]{7,5,6,4,3,2,1,0:T(8,128)(2,1)S(1)} %copy.66) | copy-start | bytes 294916
  29.1 5.2 %copy-start.24 = (bf16[1,2,1,16,1,16,1,96]{7,5,6,4,3,2,1,0:T(8,128)(2,1)}, bf16[1,2,1,16,1,16,1,96]{7,5,6,4,3,2,1,0:T(8,128)(2,1)S(1)}, u32[]{:S(2)}) copy-start(bf16[1,2,1,16,1,16,1,96]{7,5,6,4,3,2,1,0:T(8,128)(2,1)S(1)} %copy.67) | copy-start | bytes 294916
  29.2 5.4 %copy-start.22 = (bf16[1,2,1,16,1,16,1,96]{7,5,6,4,3,2,1,0:T(8,128)(2,1)}, bf16[1,2,1,16,1,16,1,96]{7,5,6,4,3,2,1,0:T(8,128)(2,1)S(1)}, u32[]{:S(2)}) copy-start(bf16[1,2,1,16,1,16,1,96]{7,5,6,4,3,2,1,0:T(8,128)(2,1)S(1)} %copy.68) | copy-start | bytes 294916
  29.2 5.6 %copy-start.20 = (bf16[1,2,1,16,1,16,1,96]{7,5,6,4,3,2,1,0:T(8,128)(2,1)}, bf16[1,2,1,16,1,16,1,96]{7,5,6,4,3,2,1,0:T(8,128)(2,1)S(1)}, u32[]{:S(2)}) copy-start(bf16[1,2,1,16,1,16,1,96]{7,5,6,4,3,2,1,0:T(8,128)(2,1)S(1)} %copy.69) | copy-start | bytes 294916
  29.2 5.8 %copy-start.18 = (bf16[1,2,1,16,1,16,1,96]{7,5,6,4,3,2,1,0:T(8,128)(2,1)}, bf16[1,2,1,16,1,16,1,96]{7,5,6,4,3,2,1,0:T(8,128)(2,1)S(1)}, u32[]{:S(2)}) copy-start(bf16[1,2,1,16,1,16,1,96]{7,5,6,4,3,2,1,0:T(8,128)(2,1)S(1)} %copy.70) | copy-start | bytes 294916
  29.3 6.1 %copy-start.16 = (bf16[1,2,1,16,1,16,1,96]{7,5,6,4,3,2,1,0:T(8,128)(2,1)}, bf16[1,2,1,16,1,16,1,96]{7,5,6,4,3,2,1,0:T(8,128)(2,1)S(1)}, u32[]{:S(2)}) copy-start(bf16[1,2,1,16,1,16,1,96]{7,5,6,4,3,2,1,0:T(8,128)(2,1)S(1)} %copy.71) | copy-start | bytes 294916
  29.3 6.3 %copy-start.14 = (bf16[1,2,1,16,1,16,1,96]{7,5,6,4,3,2,1,0:T(8,128)(2,1)}, bf16[1,2,1,16,1,16,1,96]{7,5,6,4,3,2,1,0:T(8,128)(2,1)S(1)}, u32[]{:S(2)}) copy-start(bf16[1,2,1,16,1,16,1,96]{7,5,6,4,3,2,1,0:T(8,128)(2,1)S(1)} %copy.72) | copy-start | bytes 294916
  29.4 6.5 %copy-start.12 = (bf16[1,2,1,16,1,16,1,96]{7,5,6,4,3,2,1,0:T(8,128)(2,1)}, bf16[1,2,1,16,1,16,1,96]{7,5,6,4,3,2,1,0:T(8,128)(2,1)S(1)}, u32[]{:S(2)}) copy-start(bf16[1,2,1,16,1,16,1,96]{7,5,6,4,3,2,1,0:T(8,128)(2,1)S(1)} %copy.73) | copy-start | bytes 294916
  29.4 6.8 %copy-start.10 = (bf16[1,2,1,16,1,16,1,96]{7,5,6,4,3,2,1,0:T(8,128)(2,1)}, bf16[1,2,1,16,1,16,1,96]{7,5,6,4,3,2,1,0:T(8,128)(2,1)S(1)}, u32[]{:S(2)}) copy-start(bf16[1,2,1,16,1,16,1,96]{7,5,6,4,3,2,1,0:T(8,128)(2,1)S(1)} %copy.74) | copy-start | bytes 294916
  29.4 7.0 %copy-start.8 = (bf16[1,2,1,16,1,16,1,96]{7,5,6,4,3,2,1,0:T(8,128)(2,1)}, bf16[1,2,1,16,1,16,1,96]{7,5,6,4,3,2,1,0:T(8,128)(2,1)S(1)}, u32[]{:S(2)}) copy-start(bf16[1,2,1,16,1,16,1,96]{7,5,6,4,3,2,1,0:T(8,128)(2,1)S(1)} %copy.75) | copy-start | bytes 294916
  29.5 7.2 %copy-start.6 = (bf16[1,2,1,16,1,16,1,96]{7,5,6,4,3,2,1,0:T(8,128)(2,1)}, bf16[1,2,1,16,1,16,1,96]{7,5,6,4,3,2,1,0:T(8,128)(2,1)S(1)}, u32[]{:S(2)}) copy-start(bf16[1,2,1,16,1,16,1,96]{7,5,6,4,3,2,1,0:T(8,128)(2,1)S(1)} %copy.76) | copy-start | bytes 294916
  29.5 7.5 %copy-start.4 = (bf16[1,2,1,16,1,16,1,96]{7,5,6,4,3,2,1,0:T(8,128)(2,1)}, bf16[1,2,1,16,1,16,1,96]{7,5,6,4,3,2,1,0:T(8,128)(2,1)S(1)}, u32[]{:S(2)}) copy-start(bf16[1,2,1,16,1,16,1,96]{7,5,6,4,3,2,1,0:T(8,128)(2,1)S(1)} %copy.77) | copy-start | bytes 294916
  29.6 8.4 %copy-start.48 = (bf16[1,2,1,16,1,16,1,96]{7,5,6,4,3,2,1,0:T(8,128)(2,1)}, bf16[1,2,1,16,1,16,1,96]{7,5,6,4,3,2,1,0:T(8,128)(2,1)S(1)}, u32[]{:S(2)}) copy-start(bf16[1,2,1,16,1,16,1,96]{7,5,6,4,3,2,1,0:T(8,128)(2,1)S(1)} %copy.81) | copy-start | bytes 294916
  38.8 3.4 %copy-start.47 = (bf16[1,2,1,16,1,16,1,96]{7,5,6,4,3,2,1,0:T(8,128)(2,1)S(1)}, bf16[1,2,1,16,1,16,1,96]{7,5,6,4,3,2,1,0:T(8,128)(2,1)}, u32[]{:S(2)}) copy-start(bf16[1,2,1,16,1,16,1,96]{7,5,6,4,3,2,1,0:T(8,128)(2,1)} %copy-done.46) | copy-start | bytes 294916
  38.8 3.7 %copy-start.45 = (bf16[1,2,1,16,1,16,1,96]{7,5,6,4,3,2,1,0:T(8,128)(2,1)S(1)}, bf16[1,2,1,16,1,16,1,96]{7,5,6,4,3,2,1,0:T(8,128)(2,1)}, u32[]{:S(2)}) copy-start(bf16[1,2,1,16,1,16,1,96]{7,5,6,4,3,2,1,0:T(8,128)(2,1)} %copy-done.44) | copy-start | bytes 294916
  38.8 3.9 %copy-start.43 = (bf16[1,2,1,16,1,16,1,96]{7,5,6,4,3,2,1,0:T(8,128)(2,1)S(1)}, bf16[1,2,1,16,1,16,1,96]{7,5,6,4,3,2,1,0:T(8,128)(2,1)}, u32[]{:S(2)}) copy-start(bf16[1,2,1,16,1,16,1,96]{7,5,6,4,3,2,1,0:T(8,128)(2,1)} %copy-done.42) | copy-start | bytes 294916
  39.7 3.6 %copy-start.39 = (bf16[1,2,1,16,1,16,1,96]{7,5,6,4,3,2,1,0:T(8,128)(2,1)S(1)}, bf16[1,2,1,16,1,16,1,96]{7,5,6,4,3,2,1,0:T(8,128)(2,1)}, u32[]{:S(2)}) copy-start(bf16[1,2,1,16,1,16,1,96]{7,5,6,4,3,2,1,0:T(8,128)(2,1)} %copy-done.38) | copy-start | bytes 294916
  39.7 3.8 %copy-start.35 = (bf16[1,2,1,16,1,16,1,96]{7,5,6,4,3,2,1,0:T(8,128)(2,1)S(1)}, bf16[1,2,1,16,1,16,1,96]{7,5,6,4,3,2,1,0:T(8,128)(2,1)}, u32[]{:S(2)}) copy-start(bf16[1,2,1,16,1,16,1,96]{7,5,6,4,3,2,1,0:T(8,128)(2,1)} %copy-done.34) | copy-start | bytes 294916
  39.9 3.9 %copy-start.37 = (bf16[1,2,1,16,1,16,1,96]{7,5,6,4,3,2,1,0:T(8,128)(2,1)S(1)}, bf16[1,2,1,16,1,16,1,96]{7,5,6,4,3,2,1,0:T(8,128)(2,1)}, u32[]{:S(2)}) copy-start(bf16[1,2,1,16,1,16,1,96]{7,5,6,4,3,2,1,0:T(8,128)(2,1)} %copy-done.36) | copy-start | bytes 294916
  39.9 4.1 %copy-start.33 = (bf16[1,2,1,16,1,16,1,96]{7,5,6,4,3,2,1,0:T(8,128)(2,1)S(1)}, bf16[1,2,1,16,1,16,1,96]{7,5,6,4,3,2,1,0:T(8,128)(2,1)}, u32[]{:S(2)}) copy-start(bf16[1,2,1,16,1,16,1,96]{7,5,6,4,3,2,1,0:T(8,128)(2,1)} %copy-done.32) | copy-start | bytes 294916
  40.6 12.9 %collective-permute-start.1 = (bf16[1,1,16,16,192]{4,3,2,1,0:T(8,128)(2,1)}, bf16[1,1,16,16,192]{4,3,2,1,0:T(8,128)(2,1)S(1)}, u32[]{:S(2)}, u32[]{:S(2)}) collective-permute-start(bf16[1,1,16,16,192]{4,3,2,1,0:T(8,128)(2,1)} %slice.310), channel_id=1, source_target_pairs={{1,0},{2,1},{3,2},{4,3},{5,4},{6,5},{7,6},{8,7},{9,8},{10,9},{11,1... | collective-permute-start | bytes 294920 | tf_op jit(solution)/shard_map/ppermute | solution.py:19
  53.4 221.3 %all-reduce.32.cloned.1.call-start = ((), (), s32[]{:S(2)}) async-start(), calls=%async_computation | async-start | bytes 442368 | tf_op jit(solution)/shard_map/psum | solution.py:135
  (24 other events, 49.7 us)
Sparse Core Ops, SparseCore 0:
  53.5 123.1 all-reduce.33
  180.8 93.8 all-reduce.31

commit v2 on v1

v2 whole, which is shorter than its diff:
```python
import functools

import jax
import jax.numpy as jnp
import numpy as np
from jax import lax
from jax.experimental import pallas as pl
from jax.experimental.pallas import tpu as pltpu
from jax.sharding import PartitionSpec as P

F32, BF16 = jnp.float32, jnp.bfloat16
MESH = pl.DeviceIdType.MESH

NY, NX, NZ = 4, 4, 8
PEERS = NY * NX
COUT = 192
LANES = 3072
PAIRS = 8
WIN = 384
HALF = COUT // 2
MINE = 12
CHUNK = 256
NT = (((1,), (1,)), ((), ()))


def dot(a, b, dims=(((1,), (0,)), ((), ()))):
    return lax.dot_general(a, b, dims, preferred_element_type=F32)


def kernel(
    x_hbm, w_hbm, cot_hbm, perm_hbm,
    act_hbm, grad_hbm, wg_hbm,
    x_in, x_halo, w_in, cot_in, perm,
    rows_f32, rows_bf, w_par, gs, part, part_bf, core_in,
    own, chunks, chunk_in, z_out, z_in, gathered, dx, act, grad, wg,
    load_sem, store_sem, halo_send, halo_recv, core_send, core_recv,
    xy_send, xy_recv, z_send, z_recv, ag_send, ag_recv,
):
    sample, space = lax.axis_index("sample"), lax.axis_index("space")
    y, x = sample // NX, sample % NX
    z, core = space // 2, space % 2
    after = {"space": (space + 1) % (2 * NZ)}
    before = {"space": (space + 2 * NZ - 1) % (2 * NZ)}
    other = {"space": z * 2 + (1 - core)}

    def plane(k):
        dy, dx_ = k // NX, k % NX
        return ((y + dy) % NY) * NX + (x + dx_) % NX

    def depth(k):
        return {"space": ((z + k) % NZ) * 2 + core}

    loads = [
        pltpu.make_async_copy(src, dst, load_sem.at[n])
        for n, (src, dst) in enumerate(
            ((x_hbm, x_in), (w_hbm, w_in), (cot_hbm, cot_in), (perm_hbm, perm))
        )
    ]
    for load in loads:
        load.start()

    barrier = pltpu.get_barrier_semaphore()
    for device in [after, before] + [depth(k) for k in range(1, NZ)] + [
        {"sample": plane(k)} for k in range(1, PEERS)
    ]:
        pl.semaphore_signal(barrier, inc=1, device_id=device, device_id_type=MESH)

    rows_f32[:, :, 0:8, :] = jnp.zeros((5, 24, 8, 128), F32)
    rows_bf[:, :, :, 0:128] = jnp.zeros((3, 5, 16, 128), BF16)

    loads[0].wait()
    pl.semaphore_wait(barrier, 2 + NZ - 1 + PEERS - 1)
    x_copy = pltpu.make_async_remote_copy(
        src_ref=x_in.at[3], dst_ref=x_halo, send_sem=halo_send.at[0], recv_sem=halo_recv.at[0],
        device_id=after, device_id_type=MESH,
    )
    x_copy.start()

    def split_rows(d, values):
        for t in range(24):
            rows_f32[d, t, 8:40] = values[:, 128 * t : 128 * t + 128].astype(F32)
        for t in range(24):
            for b in range(3):
                piece = rows_f32[d, t, pl.ds(7 + b, 16, stride=2), :]
                rows_bf[b, d, :, 128 * t + 128 : 128 * t + 256] = piece.astype(BF16)

    for d in range(4):
        split_rows(d + 1, x_in[d])

    loads[1].wait()
    w_par[...] = jnp.zeros(w_par.shape, BF16)
    w_par[0, :, 32:320, 0:COUT] = w_in[...]
    w_par[1, :, 96:384, 0:COUT] = w_in[...]
    chunks[PEERS - 3 :] = jnp.zeros((3, HALF, CHUNK), BF16)
    own[PEERS - 3 :] = jnp.zeros((3, HALF, CHUNK), F32)

    def windows(par, a, b):
        return jnp.concatenate(
            [
                rows_bf[b, a + 2 * i, :, 384 * m + 128 * par : 384 * m + 128 * par + WIN]
                for i in range(2)
                for m in range(PAIRS)
            ],
            axis=0,
        )

    pre = [None, None]
    for a in (1, 2, 0):
        if a == 0:
            x_copy.wait()
            halo = x_halo[...]
            split_rows(0, jnp.where(space == 0, jnp.zeros_like(halo), halo))
        for par in range(2):
            for b in range(3):
                term = dot(windows(par, a, b), w_par[par, 3 * a + b])
                pre[par] = term if pre[par] is None else pre[par] + term

    loads[2].wait()
    activation = []
    for par in range(2):
        cot = jnp.concatenate(
            [
                cot_in[i, :, 384 * m + 128 * par : 384 * m + 128 * par + 256]
                for i in range(2)
                for m in range(PAIRS)
            ],
            axis=0,
        ).astype(F32)
        if par == 1:
            cot = pltpu.roll(cot, 192, 1)
        sigmoid_val = jax.nn.sigmoid(pre[par])
        activation.append(pre[par] * sigmoid_val)
        g = cot * (sigmoid_val * (1.0 + pre[par] * (1.0 - sigmoid_val)))
        g = g.astype(BF16)
        for i in range(2):
            gs[i, par] = g[128 * i : 128 * i + 128]
    g_copy = pltpu.make_async_remote_copy(
        src_ref=gs.at[0], dst_ref=gs.at[2], send_sem=halo_send.at[1], recv_sem=halo_recv.at[1],
        device_id=before, device_id_type=MESH,
    )
    g_copy.start()

    loads[3].wait()
    turned = [
        dot(perm[...], jnp.concatenate([gs[0, par], gs[1, par]], axis=0), NT).astype(BF16)
        for par in range(2)
    ]
    core_copies = []
    for tap in range(9):
        lanes = pl.ds(WIN * tap, WIN)
        total = dot(turned[0], windows(0, tap // 3, tap % 3)) + pltpu.roll(
            dot(turned[1], windows(1, tap // 3, tap % 3)), WIN - 64, 1
        )
        part[:, lanes] = total
        part_bf[:, lanes] = total.astype(BF16)
        copy = pltpu.make_async_remote_copy(
            src_ref=part_bf.at[pl.ds(pl.multiple_of((1 - core) * HALF, HALF), HALF), lanes],
            dst_ref=core_in.at[:, lanes],
            send_sem=core_send.at[tap], recv_sem=core_recv.at[tap],
            device_id=other, device_id_type=MESH,
        )
        copy.start()
        core_copies.append(copy)

    mine = pl.ds(pl.multiple_of(core * HALF, HALF), HALF)
    for tap in range(9):
        core_copies[tap].wait()
        lanes = pl.ds(WIN * tap, WIN)
        total = part[mine, lanes] + core_in[:, lanes].astype(F32)
        for u in range(3):
            t = 3 * tap + u
            piece = total[:, 128 * u : 128 * u + 128]
            own[t // 2, :, 128 * (t % 2) : 128 * (t % 2) + 128] = piece
            chunks[t // 2, :, 128 * (t % 2) : 128 * (t % 2) + 128] = piece.astype(BF16)

    xy_copies = []
    for k in range(1, PEERS):
        copy = pltpu.make_async_remote_copy(
            src_ref=chunks.at[plane(k)], dst_ref=chunk_in.at[k - 1],
            send_sem=xy_send.at[k - 1], recv_sem=xy_recv.at[k - 1],
            device_id={"sample": plane(k)}, device_id_type=MESH,
        )
        copy.start()
        xy_copies.append(copy)

    low = lax.broadcasted_iota(jnp.int32, (256, 128), 1) < 64
    moved = pltpu.roll(activation[1], 64, 1)
    middle = jnp.where(low, activation[0][:, 128:], moved[:, :128])
    dense = jnp.concatenate([activation[0][:, :128], middle, moved[:, 128:]], axis=1).astype(BF16)
    for i in range(2):
        for m in range(PAIRS):
            row = 128 * i + 16 * m
            act[i, :, 384 * m : 384 * m + 384] = dense[row : row + 16]
    act_store = pltpu.make_async_copy(act, act_hbm, store_sem.at[0])
    act_store.start()

    row = lax.broadcasted_iota(jnp.int32, (128, 256), 0)
    last_row = row % 16 == 15

    def shifted(value):
        up = pltpu.roll(value.astype(F32), 127, 0)
        return jnp.where(last_row, 0.0, up).astype(BF16)

    g_copy.wait()
    g_rows = [[gs[i, par] for par in range(2)] for i in range(3)]
    outside = space == 2 * NZ - 1
    for par in range(2):
        g_rows[2][par] = jnp.where(outside, jnp.zeros_like(g_rows[2][par]), g_rows[2][par])
    g_shift = [[shifted(g_rows[i][par]) for par in range(2)] for i in range(3)]

    def terms(par, first, row_par, a):
        def both(source):
            return jnp.concatenate([source[first][par], source[first + 1][par]], axis=0)

        if row_par == 0:
            return dot(both(g_rows), w_par[par, 3 * a + 1], NT)
        return dot(both(g_rows), w_par[par, 3 * a + 2], NT) + dot(
            both(g_shift), w_par[par, 3 * a], NT
        )

    for depth_par in range(2):
        for row_par in range(2):
            sums = []
            for par in range(2):
                if depth_par == 0:
                    sums.append(terms(par, 0, row_par, 1))
                else:
                    sums.append(terms(par, 0, row_par, 2) + terms(par, 1, row_par, 0))
            for i in range(2):
                for m in range(PAIRS):
                    at = 128 * i + 16 * m
                    value = sums[1][at : at + 16]
                    left = sums[0][at : at + 16, 128:]
                    if m < PAIRS - 1:
                        right = sums[0][at + 16 : at + 32, :128]
                    else:
                        right = jnp.zeros((16, 128), F32)
                    value = value + jnp.concatenate([left, right], axis=1)
                    for u in range(3):
                        piece = value[:, 128 * u : 128 * u + 128]
                        dx[2 * i + depth_par, 3 * m + u, pl.ds(row_par, 16, stride=2), :] = piece
    for d in range(4):
        for t in range(24):
            grad[d, :, 128 * t : 128 * t + 128] = dx[d, t].astype(BF16)
    grad_store = pltpu.make_async_copy(grad, grad_hbm, store_sem.at[1])
    grad_store.start()

    for copy in xy_copies:
        copy.wait()
    total = own[sample]
    for k in range(PEERS - 1):
        total = total + chunk_in[k].astype(F32)
    for k in range(NZ):
        z_out[k, 0:MINE] = total[MINE * k : MINE * k + MINE]
        z_out[k, MINE:16] = jnp.zeros((16 - MINE, CHUNK), F32)

    z_copies = []
    for k in range(1, NZ):
        copy = pltpu.make_async_remote_copy(
            src_ref=z_out.at[(z + k) % NZ], dst_ref=z_in.at[k - 1],
            send_sem=z_send.at[k - 1], recv_sem=z_recv.at[k - 1],
            device_id=depth(k), device_id_type=MESH,
        )
        copy.start()
        z_copies.append(copy)
    for copy in z_copies:
        copy.wait()
    total = z_out[z]
    for k in range(NZ - 1):
        total = total + z_in[k]
    gathered[sample] = total * (1.0 / PEERS)

    ag_copies = []
    for k in range(1, PEERS):
        copy = pltpu.make_async_remote_copy(
            src_ref=gathered.at[sample], dst_ref=gathered.at[sample],
            send_sem=ag_send.at[k - 1], recv_sem=ag_recv.at[k - 1],
            device_id={"sample": plane(k)}, device_id_type=MESH,
        )
        copy.start()
        ag_copies.append(copy)
    for copy in ag_copies:
        copy.wait()
    for tap in range(9):
        window = jnp.concatenate(
            [
                gathered[t // 2, :, 128 * (t % 2) : 128 * (t % 2) + 128]
                for t in range(3 * tap, 3 * tap + 3)
            ],
            axis=1,
        )
        for e in range(3):
            wg[3 * tap + e] = window[0:MINE, 32 + 96 * e : 128 + 96 * e]
    wg_store = pltpu.make_async_copy(wg, wg_hbm, store_sem.at[2])
    wg_store.start()
    act_store.wait()
    grad_store.wait()
    wg_store.wait()


def channel_order():
    table = np.zeros((COUT, 256), np.float32)
    for r in range(COUT):
        c, rest = divmod(r, HALF)
        zz, t = divmod(rest, MINE)
        table[r, (2 * zz + c) * MINE + t] = 1.0
    return jnp.asarray(table, BF16)


def per_device(slabs, weight, cotangent):
    any_space = pl.BlockSpec(memory_space=pl.ANY)
    dma = pltpu.SemaphoreType.DMA
    activation, input_grad, gradient = pl.pallas_call(
        kernel,
        out_shape=(
            jax.ShapeDtypeStruct((2, 16, LANES), BF16),
            jax.ShapeDtypeStruct((4, 32, LANES), BF16),
            jax.ShapeDtypeStruct((27, MINE, 96), F32),
        ),
        in_specs=[any_space] * 4,
        out_specs=(any_space,) * 3,
        scratch_shapes=[
            pltpu.VMEM((4, 32, LANES), BF16),
            pltpu.VMEM((32, LANES), BF16),
            pltpu.VMEM((9, 288, COUT), BF16),
            pltpu.VMEM((2, 16, LANES), BF16),
            pltpu.VMEM((COUT, 256), BF16),
            pltpu.VMEM((5, 24, 40, 128), F32),
            pltpu.VMEM((3, 5, 16, LANES + 128), BF16),
            pltpu.VMEM((2, 9, WIN, 256), BF16),
            pltpu.VMEM((3, 2, 128, 256), BF16),
            pltpu.VMEM((COUT, 9 * WIN), F32),
            pltpu.VMEM((COUT, 9 * WIN), BF16),
            pltpu.VMEM((HALF, 9 * WIN), BF16),
            pltpu.VMEM((PEERS, HALF, CHUNK), F32),
            pltpu.VMEM((PEERS, HALF, CHUNK), BF16),
            pltpu.VMEM((PEERS - 1, HALF, CHUNK), BF16),
            pltpu.VMEM((NZ, 16, CHUNK), F32),
            pltpu.VMEM((NZ - 1, 16, CHUNK), F32),
            pltpu.VMEM((PEERS, 16, CHUNK), F32),
            pltpu.VMEM((4, 24, 32, 128), F32),
            pltpu.VMEM((2, 16, LANES), BF16),
            pltpu.VMEM((4, 32, LANES), BF16),
            pltpu.VMEM((27, MINE, 96), F32),
            dma((4,)), dma((3,)), dma((2,)), dma((2,)), dma((9,)), dma((9,)),
            dma((PEERS - 1,)), dma((PEERS - 1,)), dma((NZ - 1,)), dma((NZ - 1,)),
            dma((PEERS - 1,)), dma((PEERS - 1,)),
        ],
        compiler_params=pltpu.CompilerParams(
            collective_id=0, has_side_effects=True, vmem_limit_bytes=60 << 20
        ),
        name="conv_layer",
    )(
        slabs.reshape(4, 32, LANES),
        weight.reshape(9, 288, COUT),
        cotangent.reshape(2, 16, LANES),
        channel_order(),
    )
    return (
        activation.reshape(1, 2, 16, LANES),
        input_grad.reshape(1, 4, 32, LANES),
        jnp.swapaxes(gradient, 1, 2).reshape(3, 3, 3, 96, MINE),
    )


def solution(mesh):
    placed = (P("sample", "space", None, None), P(), P("sample", "space", None, None))
    return jax.shard_map(
        per_device,
        mesh=mesh,
        in_specs=placed,
        out_specs=(
            P("sample", "space", None, None),
            P("sample", "space", None, None),
            P(None, None, None, None, "space"),
        ),
        check_vma=False,
    )
```

time: 285 us -> 49.8 us (0.17)
  waiting for transfers between devices: 197 us -> 0 us
  Pallas kernels: 0 us -> 44.4 us
  local copies, waits for them, and re-layouts: 37 us -> 4.41 us
  matrix products: 20 us -> 0 us
  between operations: 16.4 us -> 0.65 us
  other arithmetic: 9.36 us -> 0 us
  starting transfers between devices: 3.29 us -> 0 us
    unnamed x3 -> x0, waiting for transfers between devices: 110 us -> none
    psum x1 -> x0, waiting for transfers between devices: 87 us -> none  [per_device(): gradient = lax.psum(gradient, 'sample') / lax.axis_size('sample')]
    pallas_call x0 -> x1, Pallas kernels: none -> 44.4 us  [per_device(): pl.pallas_call(kernel, out_shape=(jax.ShapeDtypeStruct((2, 16, LANES), BF...]
    dot_general x81 -> x0, matrix products: 20 us -> none  [the longest x27 7.21 us: padded_input_grad(): jnp.dot(grad_rows, weight[depth_off, row_off, col_off].T, preferred_eleme...]
    reshape x6 -> x0, local copies, waits for them, and re-layouts: 15.6 us -> none  [the longest x1 4.45 us: padded_input_grad(): jnp.stack(ordered)]
    slice x6 -> x0, local copies, waits for them, and re-layouts: 8.39 us -> none  [the longest x2 5.92 us: window_rows(): parity[:, depth_off // 2:depth_off // 2 + out_d, depth_off % 2, row_off /...]
    unnamed x7 -> x0, other arithmetic: 6.64 us -> none
    convert_element_type x3 -> x0, local copies, waits for them, and re-layouts: 4.12 us -> none  [per_device(): cotangent.reshape(preact.shape).astype(jnp.float32) * derivative(preact)]
  transfers between devices with their start and end apart: 4 -> 0, of which waited for: 2 -> 0; matrix products, arithmetic and copies ran while one was open for 13% -> 0% of each run, Pallas kernels for 0% -> 0%
where the time goes in v2:
time: 49.8 us; the launch traced here: 49.5 us
  Pallas kernels  44.4 us (89%)
  local copies, waits for them, and re-layouts  4.41 us (9%)
  between operations  0.65 us (1%)
    pallas_call x1, Pallas kernels, per_device(): pl.pallas_call(kernel, out_shape=(jax.ShapeDtypeStruct((2, 16, LANES), BF...  44.4 us
    unnamed x5, local copies, waits for them, and re-layouts  4.41 us

profile of v2, /device:TPU:2, one launch (start us, length us, event | category | flops | bytes accessed | tf_op | source)
XLA Modules:
  0.0 49.5 jit_solution(11895808679253142269)
XLA Ops:
  0.6 44.4 %conv_layer.1 = (bf16[2,16,3072]{2,1,0:T(8,128)(2,1)}, bf16[4,32,3072]{2,1,0:T(8,128)(2,1)}, f32[27,12,96]{2,1,0:T(8,128)}) custom-call(bf16[4,32,3072]{2,1,0:T(8,128)(2,1)} %bitcast.10, bf16[9,288,192]{2,1,0:T(8,128)(2,1)} %bitcast.8, bf16[2,16,3072]{2,1,0:T(8,128)(2,1)} %bitcast.12, bf16[192,256]{1,0:T(8,128)(2,1)} %constant.2.clone.perm_hbm), custom_call_target="tpu_custom_call" | custom-call | tf_op jit(solution)/shard_map/conv_layer/pallas_call | solution.py:313
  45.1 0.0 copy-start
  45.1 1.7 %copy.10 = bf16[1,2,16,3072]{3,2,1,0:T(8,128)(2,1)} copy(bf16[1,2,16,3072]{3,2,1,0:T(8,128)(2,1)} %bitcast.13) | data formatting | bytes 393216
  46.7 2.1 %copy.11 = bf16[1,4,32,3072]{3,2,1,0:T(8,128)(2,1)} copy(bf16[1,4,32,3072]{3,2,1,0:T(8,128)(2,1)} %bitcast.9) | data formatting | bytes 1572864
  48.8 0.0 copy-done
  48.8 0.7 %copy.12 = f32[3,3,3,96,12]{3,4,2,1,0:T(8,128)} copy(f32[3,3,3,96,12]{3,4,2,1,0:T(8,128)S(1)} %bitcast.11) | data formatting | bytes 248832
Async XLA Ops:
  45.1 3.7 %copy-start = (f32[27,12,96]{2,1,0:T(8,128)S(1)}, f32[27,12,96]{2,1,0:T(8,128)}, u32[]{:S(2)}) copy-start(f32[27,12,96]{2,1,0:T(8,128)} %get-tuple-element.8) | copy-start | bytes 373252

commit v3 on v2

--- a/solution.py
+++ b/solution.py
@@ -19,7 +19,8 @@
 WIN = 384
 HALF = COUT // 2
 MINE = 12
-CHUNK = 256
+TILES = 21
+UNITS = 8
 NT = (((1,), (1,)), ((), ()))
 
 
@@ -29,11 +30,11 @@
 
 def kernel(
     x_hbm, w_hbm, cot_hbm, perm_hbm,
-    act_hbm, grad_hbm, wg_hbm,
+    act, grad, wg,
     x_in, x_halo, w_in, cot_in, perm,
     rows_f32, rows_bf, w_par, gs, part, part_bf, core_in,
-    own, chunks, chunk_in, z_out, z_in, gathered, dx, act, grad, wg,
-    load_sem, store_sem, halo_send, halo_recv, core_send, core_recv,
+    own, chunks, chunk_in, summed, z_out, z_in, gathered, dx,
+    load_sem, halo_send, halo_recv, core_send, core_recv,
     xy_send, xy_recv, z_send, z_recv, ag_send, ag_recv,
 ):
     sample, space = lax.axis_index("sample"), lax.axis_index("space")
@@ -91,8 +92,8 @@
     w_par[...] = jnp.zeros(w_par.shape, BF16)
     w_par[0, :, 32:320, 0:COUT] = w_in[...]
     w_par[1, :, 96:384, 0:COUT] = w_in[...]
-    chunks[PEERS - 3 :] = jnp.zeros((3, HALF, CHUNK), BF16)
-    own[PEERS - 3 :] = jnp.zeros((3, HALF, CHUNK), F32)
+    chunks[PEERS - 1, 96:128] = jnp.zeros((32, 128), BF16)
+    own[PEERS - 1, 96:128] = jnp.zeros((32, 128), F32)
 
     def windows(par, a, b):
         return jnp.concatenate(
@@ -163,15 +164,30 @@
         core_copies.append(copy)
 
     mine = pl.ds(pl.multiple_of(core * HALF, HALF), HALF)
+
+    def place(tile, value):
+        for block in range(6):
+            unit = 6 * tile + block
+            at = 16 * (unit % UNITS)
+            own[unit // UNITS, at : at + 16] = value[16 * block : 16 * block + 16]
+            chunks[unit // UNITS, at : at + 16] = value[16 * block : 16 * block + 16].astype(BF16)
+
+    quarter = lax.broadcasted_iota(jnp.int32, (HALF, 128), 1) // 32
+    shared = None
     for tap in range(9):
         core_copies[tap].wait()
         lanes = pl.ds(WIN * tap, WIN)
         total = part[mine, lanes] + core_in[:, lanes].astype(F32)
-        for u in range(3):
-            t = 3 * tap + u
-            piece = total[:, 128 * u : 128 * u + 128]
-            own[t // 2, :, 128 * (t % 2) : 128 * (t % 2) + 128] = piece
-            chunks[t // 2, :, 128 * (t % 2) : 128 * (t % 2) + 128] = piece.astype(BF16)
+        total = pltpu.roll(total, WIN - 32, 1)
+        place(2 * tap, total[:, 0:128])
+        place(2 * tap + 1, total[:, 128:256])
+        rest = total[:, 256:384]
+        if tap % 4 == 0:
+            shared = rest
+        else:
+            shared = jnp.where(quarter == tap % 4, pltpu.roll(rest, 32 * (tap % 4), 1), shared)
+        if tap % 4 == 3 or tap == 8:
+            place(18 + tap // 4, shared)
 
     xy_copies = []
     for k in range(1, PEERS):
@@ -191,8 +207,6 @@
         for m in range(PAIRS):
             row = 128 * i + 16 * m
             act[i, :, 384 * m : 384 * m + 384] = dense[row : row + 16]
-    act_store = pltpu.make_async_copy(act, act_hbm, store_sem.at[0])
-    act_store.start()
 
     row = lax.broadcasted_iota(jnp.int32, (128, 256), 0)
     last_row = row % 16 == 15
@@ -242,17 +256,16 @@
     for d in range(4):
         for t in range(24):
             grad[d, :, 128 * t : 128 * t + 128] = dx[d, t].astype(BF16)
-    grad_store = pltpu.make_async_copy(grad, grad_hbm, store_sem.at[1])
-    grad_store.start()
 
     for copy in xy_copies:
         copy.wait()
     total = own[sample]
     for k in range(PEERS - 1):
         total = total + chunk_in[k].astype(F32)
+    summed[...] = total
     for k in range(NZ):
-        z_out[k, 0:MINE] = total[MINE * k : MINE * k + MINE]
-        z_out[k, MINE:16] = jnp.zeros((16 - MINE, CHUNK), F32)
+        for t in range(2):
+            z_out[k, pl.ds(t, 8, stride=2), :] = summed[pl.ds(2 * k + t, 8, stride=16), :]
 
     z_copies = []
     for k in range(1, NZ):
@@ -281,44 +294,50 @@
         ag_copies.append(copy)
     for copy in ag_copies:
         copy.wait()
+    rows = gathered[...].reshape(16 * PEERS, 128)
+
+    def tile_rows(tile):
+        return rows[MINE * tile : MINE * tile + MINE]
+
     for tap in range(9):
-        window = jnp.concatenate(
-            [
-                gathered[t // 2, :, 128 * (t % 2) : 128 * (t % 2) + 128]
-                for t in range(3 * tap, 3 * tap + 3)
-            ],
-            axis=1,
-        )
+        rest = tile_rows(18 + tap // 4)[:, 32 * (tap % 4) : 32 * (tap % 4) + 32]
+        window = jnp.concatenate([tile_rows(2 * tap), tile_rows(2 * tap + 1), rest], axis=1)
         for e in range(3):
-            wg[3 * tap + e] = window[0:MINE, 32 + 96 * e : 128 + 96 * e]
-    wg_store = pltpu.make_async_copy(wg, wg_hbm, store_sem.at[2])
-    wg_store.start()
-    act_store.wait()
-    grad_store.wait()
-    wg_store.wait()
+            wg[3 * tap + e] = window[:, 96 * e : 96 * e + 96]
+
+
+def hand_over(*refs):
+    count = len(refs) // 2
+    sems = refs[-1]
+    copies = [
+        pltpu.make_async_copy(refs[n], refs[count + n], sems.at[n]) for n in range(count)
+    ]
+    for copy in copies:
+        copy.start()
+    for copy in copies:
+        copy.wait()
 
 
 def channel_order():
     table = np.zeros((COUT, 256), np.float32)
     for r in range(COUT):
         c, rest = divmod(r, HALF)
-        zz, t = divmod(rest, MINE)
-        table[r, (2 * zz + c) * MINE + t] = 1.0
+        block, inside = divmod(rest, 16)
+        zz, t = divmod(inside, 2)
+        table[r, (2 * zz + c) * MINE + 2 * block + t] = 1.0
     return jnp.asarray(table, BF16)
 
 
 def per_device(slabs, weight, cotangent):
     any_space = pl.BlockSpec(memory_space=pl.ANY)
     dma = pltpu.SemaphoreType.DMA
-    activation, input_grad, gradient = pl.pallas_call(
+    shapes = (((2, 16, LANES), BF16), ((4, 32, LANES), BF16), ((27, MINE, 96), F32))
+    on_chip = pl.BlockSpec(memory_space=pltpu.VMEM)
+    results = pl.pallas_call(
         kernel,
-        out_shape=(
-            jax.ShapeDtypeStruct((2, 16, LANES), BF16),
-            jax.ShapeDtypeStruct((4, 32, LANES), BF16),
-            jax.ShapeDtypeStruct((27, MINE, 96), F32),
-        ),
-        in_specs=[any_space] * 4,
-        out_specs=(any_space,) * 3,
+        out_shape=tuple(pltpu.VMEM(*shape) for shape in shapes),
+        in_specs=[pl.BlockSpec(memory_space=pltpu.HBM)] * 4,
+        out_specs=(on_chip,) * 3,
         scratch_shapes=[
             pltpu.VMEM((4, 32, LANES), BF16),
             pltpu.VMEM((32, LANES), BF16),
@@ -332,30 +351,42 @@
             pltpu.VMEM((COUT, 9 * WIN), F32),
             pltpu.VMEM((COUT, 9 * WIN), BF16),
             pltpu.VMEM((HALF, 9 * WIN), BF16),
-            pltpu.VMEM((PEERS, HALF, CHUNK), F32),
-            pltpu.VMEM((PEERS, HALF, CHUNK), BF16),
-            pltpu.VMEM((PEERS - 1, HALF, CHUNK), BF16),
-            pltpu.VMEM((NZ, 16, CHUNK), F32),
-            pltpu.VMEM((NZ - 1, 16, CHUNK), F32),
-            pltpu.VMEM((PEERS, 16, CHUNK), F32),
+            pltpu.VMEM((PEERS, 128, 128), F32),
+            pltpu.VMEM((PEERS, 128, 128), BF16),
+            pltpu.VMEM((PEERS - 1, 128, 128), BF16),
+            pltpu.VMEM((128, 128), F32),
+            pltpu.VMEM((NZ, 16, 128), F32),
+            pltpu.VMEM((NZ - 1, 16, 128), F32),
+            pltpu.VMEM((PEERS, 16, 128), F32),
             pltpu.VMEM((4, 24, 32, 128), F32),
-            pltpu.VMEM((2, 16, LANES), BF16),
-            pltpu.VMEM((4, 32, LANES), BF16),
-            pltpu.VMEM((27, MINE, 96), F32),
-            dma((4,)), dma((3,)), dma((2,)), dma((2,)), dma((9,)), dma((9,)),
+            dma((4,)), dma((2,)), dma((2,)), dma((9,)), dma((9,)),
             dma((PEERS - 1,)), dma((PEERS - 1,)), dma((NZ - 1,)), dma((NZ - 1,)),
             dma((PEERS - 1,)), dma((PEERS - 1,)),
         ],
         compiler_params=pltpu.CompilerParams(
-            collective_id=0, has_side_effects=True, vmem_limit_bytes=60 << 20
+            collective_id=0, has_side_effects=True, vmem_limit_bytes=48 << 20
         ),
         name="conv_layer",
     )(
-        slabs.reshape(4, 32, LANES),
-        weight.reshape(9, 288, COUT),
-        cotangent.reshape(2, 16, LANES),
-        channel_order(),
+        *(
+            pltpu.with_memory_space_constraint(array, pltpu.HBM)
+            for array in (
+                slabs.reshape(4, 32, LANES),
+                weight.reshape(9, 288, COUT),
+                cotangent.reshape(2, 16, LANES),
+                channel_order(),
+            )
+        )
     )
+    activation, input_grad, gradient = pl.pallas_call(
+        hand_over,
+        out_shape=tuple(jax.ShapeDtypeStruct(*shape) for shape in shapes),
+        in_specs=[on_chip] * 3,
+        out_specs=(any_space,) * 3,
+        scratch_shapes=[dma((3,))],
+        compiler_params=pltpu.CompilerParams(vmem_limit_bytes=4 << 20),
+        name="hand_over",
+    )(*(pltpu.with_memory_space_constraint(array, pltpu.VMEM) for array in results))
     return (
         activation.reshape(1, 2, 16, LANES),
         input_grad.reshape(1, 4, 32, LANES),

time: 49.8 us -> 40.3 us (0.81)
  Pallas kernels: 44.4 us -> 39.5 us
  local copies, waits for them, and re-layouts: 4.41 us -> 0 us
    pallas_call x1 -> x2, Pallas kernels: 44.4 us -> 39.5 us  [the longest x1 38.4 us: per_device(): pl.pallas_call(kernel, out_shape=tuple((pltpu.VMEM(*shape) for shape in s...]
    unnamed x5 -> x0, local copies, waits for them, and re-layouts: 4.41 us -> none
where the time goes in v3:
time: 40.3 us; the launch traced here: 40.1 us
  Pallas kernels  39.5 us (98%)
  between operations  0.64 us (2%)
    pallas_call x1, Pallas kernels, per_device(): pl.pallas_call(kernel, out_shape=tuple((pltpu.VMEM(*shape) for shape in s...  38.4 us
    pallas_call x1, Pallas kernels, per_device(): pl.pallas_call(hand_over, out_shape=tuple((jax.ShapeDtypeStruct(*shape) f...  1.02 us

profile of v3, /device:TPU:2, one launch (start us, length us, event | category | flops | bytes accessed | tf_op | source)
XLA Modules:
  0.0 40.1 jit_solution(5919527677213345496)
XLA Ops:
  0.6 38.4 %conv_layer.1 = (bf16[2,16,3072]{2,1,0:T(8,128)(2,1)S(1)}, bf16[4,32,3072]{2,1,0:T(8,128)(2,1)S(1)}, f32[27,12,96]{2,1,0:T(8,128)S(1)}) custom-call(bf16[4,32,3072]{2,1,0:T(8,128)(2,1)} %bitcast.9, bf16[9,288,192]{2,1,0:T(8,128)(2,1)} %bitcast.8, bf16[2,16,3072]{2,1,0:T(8,128)(2,1)} %bitcast.10, bf16[192,256]{1,0:T(8,128)(2,1)} %constant.2.clone.perm_hbm), custom_call_target="tpu_custom_call" | custom-call | tf_op jit(solution)/shard_map/conv_layer/pallas_call | solution.py:336
  39.1 1.0 %hand_over.1 = (bf16[2,16,3072]{2,1,0:T(8,128)(2,1)}, bf16[4,32,3072]{2,1,0:T(8,128)(2,1)}, f32[27,12,96]{2,1,0:T(8,128)}) custom-call(bf16[2,16,3072]{2,1,0:T(8,128)(2,1)S(1)} %get-tuple-element.9.refs_0_, bf16[4,32,3072]{2,1,0:T(8,128)(2,1)S(1)} %get-tuple-element.10.refs_1_, f32[27,12,96]{2,1,0:T(8,128)S(1)} %get-tuple-element.11.refs_2_), custom_call_target="tpu_custom_call" | custom-call | tf_op jit(solution)/shard_map/hand_over/pallas_call | solution.py:381

commit v4 on v3

v4 whole, which is shorter than its diff:
```python
import functools

import jax
import jax.numpy as jnp
import numpy as np
from jax import lax
from jax.experimental import pallas as pl
from jax.experimental.pallas import tpu as pltpu
from jax.sharding import PartitionSpec as P

F32, BF16 = jnp.float32, jnp.bfloat16
MESH = pl.DeviceIdType.MESH

NY, NX, NZ = 4, 4, 8
PEERS = NY * NX
COUT = 192
LANES = 3072
PAIRS = 8
WIN = 384
HALF = COUT // 2
MINE = 12
TILES = 21
UNITS = 8
BLOCKS = UNITS * PEERS
NT = (((1,), (1,)), ((), ()))


def dot(a, b, dims=(((1,), (0,)), ((), ()))):
    return lax.dot_general(a, b, dims, preferred_element_type=F32)


def position():
    sample, space = lax.axis_index("sample"), lax.axis_index("space")
    after = {"space": (space + 1) % (2 * NZ)}
    before = {"space": (space + 2 * NZ - 1) % (2 * NZ)}
    return sample, space, after, before


def greet(barrier, device, exists=None):
    def signal():
        pl.semaphore_signal(barrier, inc=1, device_id=device, device_id_type=MESH)

    if exists is None:
        signal()
    else:
        pl.when(exists)(signal)


def split_rows(values, rows_f32, rows_bf, rows_sh, d):
    for t in range(24):
        rows_f32[t, 8:40] = values[:, 128 * t : 128 * t + 128].astype(F32)
    lane = lax.broadcasted_iota(jnp.int32, (16, 128), 1)
    zero = jnp.zeros((16, 128), F32)
    for b in range(3):
        pieces = [rows_f32[t, pl.ds(7 + b, 16, stride=2), :] for t in range(24)]
        for t in range(24):
            rows_bf[b, d, :, 128 * t + 128 : 128 * t + 256] = pieces[t].astype(BF16)
        for n, left in enumerate((32, 96)):
            rolled = [pltpu.roll(piece, 128 - left, 1) for piece in pieces]
            for t in range(25):
                low = rolled[t - 1] if t > 0 else zero
                high = rolled[t] if t < 24 else zero
                piece = jnp.where(lane < 128 - left, low, high)
                rows_sh[n, b, d, :, 128 * t : 128 * t + 128] = piece.astype(BF16)


def windows(rows_bf, par, d, b):
    return jnp.concatenate(
        [
            rows_bf[b, d, :, 384 * m + 128 * par : 384 * m + 128 * par + WIN]
            for m in range(PAIRS)
        ],
        axis=0,
    )


def aligned_windows(rows_sh, d, b):
    return jnp.concatenate(
        [windows(rows_sh.at[par], par, d, b) for par in range(2)], axis=0
    )


def cotangent_rows(cot_in, i, par):
    cot = jnp.concatenate(
        [
            cot_in[i, :, 384 * m + 128 * par : 384 * m + 128 * par + 256]
            for m in range(PAIRS)
        ],
        axis=0,
    ).astype(F32)
    return pltpu.roll(cot, 192, 1) if par == 1 else cot


def pointwise(pre, cot):
    sigmoid_val = jax.nn.sigmoid(pre)
    g = cot * (sigmoid_val * (1.0 + pre * (1.0 - sigmoid_val)))
    return pre * sigmoid_val, g.astype(BF16)


def side_by_side(even, odd, out):
    low = lax.broadcasted_iota(jnp.int32, (128, 128), 1) < 64
    moved = pltpu.roll(odd, 64, 1)
    middle = jnp.where(low, even[:, 128:], moved[:, :128])
    dense = jnp.concatenate([even[:, :128], middle, moved[:, 128:]], axis=1).astype(BF16)
    for m in range(PAIRS):
        out[:, 384 * m : 384 * m + 384] = dense[16 * m : 16 * m + 16]


def turn(perm, g):
    return jnp.concatenate([dot(perm[...], g[par], NT).astype(BF16) for par in range(2)], axis=1)


def first_kernel(
    x_hbm, w_hbm, cot_hbm, perm_hbm,
    x_halo, cot_in, perm, rows_sh, w_par, pre0, g1, part1, act1,
    x_in, w_in, rows_f32, rows_bf, load_sem, halo_send, halo_recv,
):
    _, space, after, before = position()
    has_before, has_after = space > 0, space < 2 * NZ - 1
    neighbours = 2 - jnp.where(has_before, 0, 1) - jnp.where(has_after, 0, 1)
    loads = [
        pltpu.make_async_copy(src, dst, load_sem.at[n])
        for n, (src, dst) in enumerate(
            ((x_hbm, x_in), (w_hbm, w_in), (cot_hbm, cot_in), (perm_hbm, perm))
        )
    ]
    for load in loads:
        load.start()
    barrier = pltpu.get_barrier_semaphore()
    @pl.when(jnp.logical_not(has_before))
    def _():
        x_halo[...] = jnp.zeros_like(x_halo)

    greet(barrier, after, has_after)
    greet(barrier, before, has_before)

    rows_f32[:, :, 0:8, :] = jnp.zeros((4, 24, 8, 128), F32)
    rows_bf[:, :, :, 0:128] = jnp.zeros((3, 5, 16, 128), BF16)
    loads[0].wait()
    pl.semaphore_wait(barrier, neighbours)
    x_copy = pltpu.make_async_remote_copy(
        src_ref=x_in.at[3], dst_ref=x_halo, send_sem=halo_send, recv_sem=halo_recv,
        device_id=after, device_id_type=MESH,
    )
    pl.when(has_after)(x_copy.start)
    for d in range(4):
        split_rows(x_in[d], rows_f32.at[d], rows_bf, rows_sh, d + 1)
    w_par[:, :, :, 128:] = jnp.zeros((2, 9, WIN, 128), BF16)
    w_par[0, :, 0:32, 0:128] = jnp.zeros((9, 32, 128), BF16)
    w_par[0, :, 320:, 0:128] = jnp.zeros((9, 64, 128), BF16)
    w_par[1, :, 0:96, 0:128] = jnp.zeros((9, 96, 128), BF16)
    loads[1].wait()
    w_par[0, :, 32:320, 0:COUT] = w_in[...]
    w_par[1, :, 96:384, 0:COUT] = w_in[...]

    pre1 = []
    for par in range(2):
        total0, total1 = None, None
        for tap in range(9):
            a, b = tap // 3, tap % 3
            high = windows(rows_bf, par, a + 2, b)
            if a == 0:
                term1 = dot(high, w_par[par, tap])
            else:
                both = dot(
                    jnp.concatenate([windows(rows_bf, par, a, b), high], axis=0), w_par[par, tap]
                )
                term1 = both[128:]
                total0 = both[:128] if total0 is None else total0 + both[:128]
            total1 = term1 if total1 is None else total1 + term1
        pre0[par] = total0
        pre1.append(total1)
    loads[2].wait()
    acts = []
    for par in range(2):
        value, g = pointwise(pre1[par], cotangent_rows(cot_in, 1, par))
        acts.append(value)
        g1[par] = g
    side_by_side(acts[0], acts[1], act1)
    loads[3].wait()
    turned = turn(perm, g1)
    for tap in range(9):
        part1[:, WIN * tap : WIN * tap + WIN] = dot(
            turned, aligned_windows(rows_sh, tap // 3 + 2, tap % 3)
        )
    pl.when(has_after)(x_copy.wait_send)
    pl.when(has_before)(x_copy.wait_recv)


def second_kernel(
    x_halo, cot_in, perm, rows_sh_in, w_par, pre0, g1, part1,
    act0, grad, wg,
    rows_f32, rows_bf, rows_sh, g0, g2, part, part_bf, core_in,
    own, chunks, chunk_in, summed, z_out, z_in, gathered, dx,
    halo_send, halo_recv, core_send, core_recv,
    xy_send, xy_recv, z_send, z_recv, ag_send, ag_recv,
):
    sample, space, after, before = position()
    has_before, has_after = space > 0, space < 2 * NZ - 1
    neighbours = 2 - jnp.where(has_before, 0, 1) - jnp.where(has_after, 0, 1)
    y, x = sample // NX, sample % NX
    z, core = space // 2, space % 2
    other = {"space": z * 2 + (1 - core)}

    def plane(k):
        return ((y + k // NX) % NY) * NX + (x + k % NX) % NX

    def depth(k):
        return {"space": ((z + k) % NZ) * 2 + core}

    def hops(k):
        return min(k // NX, NY - k // NX) + min(k % NX, NX - k % NX)

    far_first = sorted(range(1, PEERS), key=hops, reverse=True)
    far_depth = sorted(range(1, NZ), key=lambda k: min(k, NZ - k), reverse=True)

    barrier = pltpu.get_barrier_semaphore()
    peers = [(hops(k), {"sample": plane(k)}) for k in far_first]
    peers += [(min(k, NZ - k), depth(k)) for k in far_depth]
    for _, device in sorted(peers, key=lambda peer: -peer[0]):
        greet(barrier, device)
    greet(barrier, after, has_after)
    greet(barrier, before, has_before)

    @pl.when(jnp.logical_not(has_after))
    def _():
        g2[...] = jnp.zeros_like(g2)

    rows_f32[:, 0:8, :] = jnp.zeros((24, 8, 128), F32)
    rows_bf[:, :, :, 0:128] = jnp.zeros((3, 1, 16, 128), BF16)
    split_rows(x_halo[...], rows_f32, rows_bf, rows_sh, 0)
    acts = []
    for par in range(2):
        total = pre0[par]
        for b in range(3):
            total = total + dot(windows(rows_bf, par, 0, b), w_par[par, b])
        value, g = pointwise(total, cotangent_rows(cot_in, 0, par))
        acts.append(value)
        g0[par] = g
    turned = turn(perm, g0)

    quarter = lax.broadcasted_iota(jnp.int32, (COUT, 128), 1) // 32

    def full_tile(tap):
        return 9 * (tap // 4) + 2 * (tap % 4)

    def shared_tile(tap):
        return 20 if tap == 8 else 9 * (tap // 4) + 8

    def place(tile, value):
        for half in range(2):
            for block in range(6):
                at = HALF * half + 16 * block
                piece = value[at : at + 16]
                part[half, 6 * tile + block] = piece
                part_bf[half, 6 * tile + block] = piece.astype(BF16)

    for half in range(2):
        for block in range(6 * TILES, BLOCKS):
            part[half, block] = jnp.zeros((16, 128), F32)
            part_bf[half, block] = jnp.zeros((16, 128), BF16)
    shared = None
    for tap in range(9):
        a, b = tap // 3, tap % 3
        if a == 0:
            field = aligned_windows(rows_sh, 0, b)
        else:
            field = aligned_windows(rows_sh_in, a, b)
        total = part1[:, WIN * tap : WIN * tap + WIN] + dot(turned, field)
        place(full_tile(tap), total[:, 0:128])
        place(full_tile(tap) + 1, total[:, 128:256])
        rest = total[:, 256:384]
        if tap % 4 == 0:
            shared = rest
        else:
            shared = jnp.where(quarter == tap % 4, pltpu.roll(rest, 32 * (tap % 4), 1), shared)
        if tap % 4 == 3 or tap == 8:
            place(shared_tile(tap), shared)

    pl.semaphore_wait(barrier, neighbours + NZ - 1 + PEERS - 1)
    def units(c):
        return pl.ds(pl.multiple_of(UNITS * c, UNITS), UNITS)

    order = far_first + [0]
    core_copies = []
    for k in order:
        c = plane(k)
        copy = pltpu.make_async_remote_copy(
            src_ref=part_bf.at[1 - core, units(c)], dst_ref=core_in.at[units(c)],
            send_sem=core_send.at[k], recv_sem=core_recv.at[k],
            device_id=other, device_id_type=MESH,
        )
        copy.start()
        core_copies.append(copy)
    xy_copies = []
    for k, copy in zip(order, core_copies):
        copy.wait()
        c = plane(k)
        total = part[core, units(c)] + core_in[units(c)].astype(F32)
        if k == 0:
            own[...] = total
            break
        chunks[k - 1] = total.astype(BF16)
        copy = pltpu.make_async_remote_copy(
            src_ref=chunks.at[k - 1], dst_ref=chunk_in.at[k - 1],
            send_sem=xy_send.at[k - 1], recv_sem=xy_recv.at[k - 1],
            device_id={"sample": c}, device_id_type=MESH,
        )
        copy.start()
        xy_copies.append(copy)

    g_copy = pltpu.make_async_remote_copy(
        src_ref=g0, dst_ref=g2, send_sem=halo_send, recv_sem=halo_recv,
        device_id=before, device_id_type=MESH,
    )
    pl.when(has_before)(g_copy.start)
    side_by_side(acts[0], acts[1], act0)

    row = lax.broadcasted_iota(jnp.int32, (128, 256), 0)
    last_row = row % 16 == 15

    def shifted(value):
        up = pltpu.roll(value.astype(F32), 127, 0)
        return jnp.where(last_row, 0.0, up).astype(BF16)

    pl.when(has_before)(g_copy.wait_send)
    pl.when(has_after)(g_copy.wait_recv)
    g_rows = [[ref[par] for par in range(2)] for ref in (g0, g1, g2)]
    g_shift = [[shifted(g_rows[i][par]) for par in range(2)] for i in range(3)]

    def terms(par, first, row_par, a):
        def both(source):
            return jnp.concatenate([source[first][par], source[first + 1][par]], axis=0)

        if row_par == 0:
            return dot(both(g_rows), w_par[par, 3 * a + 1], NT)
        return dot(both(g_rows), w_par[par, 3 * a + 2], NT) + dot(
            both(g_shift), w_par[par, 3 * a], NT
        )

    for depth_par in range(2):
        for row_par in range(2):
            sums = []
            for par in range(2):
                if depth_par == 0:
                    sums.append(terms(par, 0, row_par, 1))
                else:
                    sums.append(terms(par, 0, row_par, 2) + terms(par, 1, row_par, 0))
            for i in range(2):
                for m in range(PAIRS):
                    at = 128 * i + 16 * m
                    value = sums[1][at : at + 16]
                    left = sums[0][at : at + 16, 128:]
                    if m < PAIRS - 1:
                        right = sums[0][at + 16 : at + 32, :128]
                    else:
                        right = jnp.zeros((16, 128), F32)
                    value = value + jnp.concatenate([left, right], axis=1)
                    for u in range(3):
                        piece = value[:, 128 * u : 128 * u + 128]
                        dx[2 * i + depth_par, 3 * m + u, pl.ds(row_par, 16, stride=2), :] = piece
    for d in range(4):
        for t in range(24):
            grad[d, :, 128 * t : 128 * t + 128] = dx[d, t].astype(BF16)

    total = own[...]
    for k, copy in zip(order, xy_copies):
        copy.wait()
        total = total + chunk_in[k - 1].astype(F32)
    summed[...] = total.reshape(16 * UNITS, 128)
    for k in range(NZ):
        for t in range(2):
            z_out[k, pl.ds(t, 8, stride=2), :] = summed[pl.ds(2 * k + t, 8, stride=16), :]

    z_copies = []
    for k in far_depth:
        copy = pltpu.make_async_remote_copy(
            src_ref=z_out.at[(z + k) % NZ], dst_ref=z_in.at[k - 1],
            send_sem=z_send.at[k - 1], recv_sem=z_recv.at[k - 1],
            device_id=depth(k), device_id_type=MESH,
        )
        copy.start()
        z_copies.append(copy)
    total = z_out[z]
    for k, copy in zip(far_depth, z_copies):
        copy.wait()
        total = total + z_in[k - 1]
    gathered[sample] = total * (1.0 / PEERS)

    ag_copies = []
    for k in far_first:
        copy = pltpu.make_async_remote_copy(
            src_ref=gathered.at[sample], dst_ref=gathered.at[sample],
            send_sem=ag_send.at[k - 1], recv_sem=ag_recv.at[k - 1],
            device_id={"sample": plane(k)}, device_id_type=MESH,
        )
        copy.start()
        ag_copies.append(copy)
    for copy in ag_copies:
        copy.wait()
    rows = gathered[...].reshape(16 * PEERS, 128)

    def tile_rows(tile):
        return rows[MINE * tile : MINE * tile + MINE]

    for tap in range(9):
        rest = tile_rows(shared_tile(tap))[:, 32 * (tap % 4) : 32 * (tap % 4) + 32]
        first = full_tile(tap)
        window = jnp.concatenate([tile_rows(first), tile_rows(first + 1), rest], axis=1)
        for e in range(3):
            wg[3 * tap + e] = window[:, 96 * e : 96 * e + 96]


def hand_over(act0, act1, grad, wg, act_hbm, grad_hbm, wg_hbm, sems):
    pairs = ((act0, act_hbm.at[0]), (act1, act_hbm.at[1]), (grad, grad_hbm), (wg, wg_hbm))
    copies = [
        pltpu.make_async_copy(src, dst, sems.at[n]) for n, (src, dst) in enumerate(pairs)
    ]
    for copy in copies:
        copy.start()
    for copy in copies:
        copy.wait()


def channel_order():
    table = np.zeros((COUT, 256), np.float32)
    for r in range(COUT):
        c, rest = divmod(r, HALF)
        block, inside = divmod(rest, 16)
        zz, t = divmod(inside, 2)
        table[r, (2 * zz + c) * MINE + 2 * block + t] = 1.0
    return jnp.asarray(table, BF16)


def per_device(slabs, weight, cotangent):
    any_space = pl.BlockSpec(memory_space=pl.ANY)
    on_chip = pl.BlockSpec(memory_space=pltpu.VMEM)
    in_hbm = pl.BlockSpec(memory_space=pltpu.HBM)
    dma = pltpu.SemaphoreType.DMA

    def held(array):
        return pltpu.with_memory_space_constraint(array, pltpu.VMEM)

    arguments = (
        slabs.reshape(4, 32, LANES),
        weight.reshape(9, 288, COUT),
        cotangent.reshape(2, 16, LANES),
        channel_order(),
    )
    *state, act1 = pl.pallas_call(
        first_kernel,
        out_shape=(
            pltpu.VMEM((32, LANES), BF16),
            pltpu.VMEM((2, 16, LANES), BF16),
            pltpu.VMEM((COUT, 256), BF16),
            pltpu.VMEM((2, 3, 5, 16, LANES + 128), BF16),
            pltpu.VMEM((2, 9, WIN, 256), BF16),
            pltpu.VMEM((2, 128, 256), F32),
            pltpu.VMEM((2, 128, 256), BF16),
            pltpu.VMEM((COUT, 9 * WIN), F32),
            pltpu.VMEM((16, LANES), BF16),
        ),
        in_specs=[in_hbm] * 4,
        out_specs=(on_chip,) * 9,
        scratch_shapes=[
            pltpu.VMEM((4, 32, LANES), BF16),
            pltpu.VMEM((9, 288, COUT), BF16),
            pltpu.VMEM((4, 24, 40, 128), F32),
            pltpu.VMEM((3, 5, 16, LANES + 128), BF16),
            dma((4,)), dma, dma,
        ],
        compiler_params=pltpu.CompilerParams(
            collective_id=0, has_side_effects=True, vmem_limit_bytes=16 << 20
        ),
        name="first_kernel",
    )(*(pltpu.with_memory_space_constraint(array, pltpu.HBM) for array in arguments))
    act0, grad, wg = pl.pallas_call(
        second_kernel,
        out_shape=(
            pltpu.VMEM((16, LANES), BF16),
            pltpu.VMEM((4, 32, LANES), BF16),
            pltpu.VMEM((27, MINE, 96), F32),
        ),
        in_specs=[on_chip] * 8,
        out_specs=(on_chip,) * 3,
        scratch_shapes=[
            pltpu.VMEM((24, 40, 128), F32),
            pltpu.VMEM((3, 1, 16, LANES + 128), BF16),
            pltpu.VMEM((2, 3, 1, 16, LANES + 128), BF16),
            pltpu.VMEM((2, 128, 256), BF16),
            pltpu.VMEM((2, 128, 256), BF16),
            pltpu.VMEM((2, BLOCKS, 16, 128), F32),
            pltpu.VMEM((2, BLOCKS, 16, 128), BF16),
            pltpu.VMEM((BLOCKS, 16, 128), BF16),
            pltpu.VMEM((UNITS, 16, 128), F32),
            pltpu.VMEM((PEERS - 1, UNITS, 16, 128), BF16),
            pltpu.VMEM((PEERS - 1, UNITS, 16, 128), BF16),
            pltpu.VMEM((128, 128), F32),
            pltpu.VMEM((NZ, 16, 128), F32),
            pltpu.VMEM((NZ - 1, 16, 128), F32),
            pltpu.VMEM((PEERS, 16, 128), F32),
            pltpu.VMEM((4, 24, 32, 128), F32),
            dma, dma, dma((PEERS,)), dma((PEERS,)),
            dma((PEERS - 1,)), dma((PEERS - 1,)), dma((NZ - 1,)), dma((NZ - 1,)),
            dma((PEERS - 1,)), dma((PEERS - 1,)),
        ],
        compiler_params=pltpu.CompilerParams(
            collective_id=1, has_side_effects=True, vmem_limit_bytes=32 << 20
        ),
        name="second_kernel",
    )(*(held(array) for array in state))
    activation, input_grad, gradient = pl.pallas_call(
        hand_over,
        out_shape=(
            jax.ShapeDtypeStruct((2, 16, LANES), BF16),
            jax.ShapeDtypeStruct((4, 32, LANES), BF16),
            jax.ShapeDtypeStruct((27, MINE, 96), F32),
        ),
        in_specs=[on_chip] * 4,
        out_specs=(any_space,) * 3,
        scratch_shapes=[dma((4,))],
        compiler_params=pltpu.CompilerParams(vmem_limit_bytes=4 << 20),
        name="hand_over",
    )(*(held(array) for array in (act0, act1, grad, wg)))
    return (
        activation.reshape(1, 2, 16, LANES),
        input_grad.reshape(1, 4, 32, LANES),
        jnp.swapaxes(gradient, 1, 2).reshape(3, 3, 3, 96, MINE),
    )


def solution(mesh):
    placed = (P("sample", "space", None, None), P(), P("sample", "space", None, None))
    return jax.shard_map(
        per_device,
        mesh=mesh,
        in_specs=placed,
        out_specs=(
            P("sample", "space", None, None),
            P("sample", "space", None, None),
            P(None, None, None, None, "space"),
        ),
        check_vma=False,
    )
```

time: 40.3 us -> 37.8 us (0.938)
  Pallas kernels: 39.5 us -> 37.1 us
    pallas_call x2 -> x3, Pallas kernels: 39.5 us -> 37.1 us  [the longest x1 31.4 us: per_device(): pl.pallas_call(second_kernel, out_shape=(pltpu.VMEM((16, LANES), BF16), p...]
where the time goes in v4:
time: 37.8 us; the launch traced here: 37.7 us
  Pallas kernels  37.1 us (98%)
  between operations  0.65 us (2%)
    pallas_call x1, Pallas kernels, per_device(): pl.pallas_call(second_kernel, out_shape=(pltpu.VMEM((16, LANES), BF16), p...  31.4 us
    pallas_call x1, Pallas kernels, per_device(): pl.pallas_call(first_kernel, out_shape=(pltpu.VMEM((32, LANES), BF16), pl...  4.62 us
    pallas_call x1, Pallas kernels, per_device(): pl.pallas_call(hand_over, out_shape=(jax.ShapeDtypeStruct((2, 16, LANES),...  1.03 us

profile of v4, /device:TPU:2, one launch (start us, length us, event | category | flops | bytes accessed | tf_op | source)
XLA Modules:
  0.0 37.7 jit_solution(11236440857908201448)
XLA Ops:
  0.6 4.6 %first_kernel.1 = (bf16[32,3072]{1,0:T(8,128)(2,1)S(1)}, bf16[2,16,3072]{2,1,0:T(8,128)(2,1)S(1)}, bf16[192,256]{1,0:T(8,128)(2,1)S(1)}, bf16[2,3,5,16,3200]{4,3...) custom-call(bf16[4,32,3072]{2,1,0:T(8,128)(2,1)} %bitcast.9, ...), custom_call_target="tpu_custom_call" | custom-call | tf_op jit(solution)/shard_map/first_kernel/pallas_call | solution.py:450
  5.3 31.4 %second_kernel.1 = (bf16[16,3072]{1,0:T(8,128)(2,1)S(1)}, bf16[4,32,3072]{2,1,0:T(8,128)(2,1)S(1)}, f32[27,12,96]{2,1,0:T(8,128)S(1)}) custom-call(bf16[32,3072]{1,0:T(8,128)(2,1)S(1)} %get-tuple-element.18.x_halo, bf16[2,16,3072]{2,1,0:T(8,128)(2,1)S(1)} %get-tuple-element.19.cot_in, bf16[192,256]{1,0:T(8,128)(2,1)S(1)} %get-tuple-element.20.perm, ...), custom_call_target="tpu_custom_call" | custom-call | tf_op jit(solution)/shard_map/second_kernel/pallas_call | solution.py:477
  36.7 1.0 %hand_over.1 = (bf16[2,16,3072]{2,1,0:T(8,128)(2,1)}, bf16[4,32,3072]{2,1,0:T(8,128)(2,1)}, f32[27,12,96]{2,1,0:T(8,128)}) custom-call(bf16[16,3072]{1,0:T(8,128)(2,1)S(1)} %get-tuple-element.26.act0, bf16[16,3072]{1,0:T(8,128)(2,1)S(1)} %get-tuple-element.27.act1, bf16[4,32,3072]{2,1,0:T(8,128)(2,1)S(1)} %get-tuple-element.28.grad, ...), custom_call_target="tpu_custom_call" | custom-call | tf_op jit(solution)/shard_map/hand_over/pallas_call | solution.py:512

commit v5 on v4

--- a/solution.py
+++ b/solution.py
@@ -34,6 +34,14 @@
     after = {"space": (space + 1) % (2 * NZ)}
     before = {"space": (space + 2 * NZ - 1) % (2 * NZ)}
     return sample, space, after, before
+
+
+def full_tile(tap):
+    return 9 * (tap // 4) + 2 * (tap % 4)
+
+
+def shared_tile(tap):
+    return 20 if tap == 8 else 9 * (tap // 4) + 8
 
 
 def greet(barrier, device, exists=None):
@@ -112,7 +120,7 @@
 
 def first_kernel(
     x_hbm, w_hbm, cot_hbm, perm_hbm,
-    x_halo, cot_in, perm, rows_sh, w_par, pre0, g1, part1, act1,
+    x_halo, cot_in, perm, rows_sh, w_par, pre0, g1, act1,
     x_in, w_in, rows_f32, rows_bf, load_sem, halo_send, halo_recv,
 ):
     _, space, after, before = position()
@@ -137,12 +145,17 @@
     rows_f32[:, :, 0:8, :] = jnp.zeros((4, 24, 8, 128), F32)
     rows_bf[:, :, :, 0:128] = jnp.zeros((3, 5, 16, 128), BF16)
     loads[0].wait()
-    pl.semaphore_wait(barrier, neighbours)
     x_copy = pltpu.make_async_remote_copy(
         src_ref=x_in.at[3], dst_ref=x_halo, send_sem=halo_send, recv_sem=halo_recv,
         device_id=after, device_id_type=MESH,
     )
-    pl.when(has_after)(x_copy.start)
+
+    def send_plane():
+        pl.semaphore_wait(barrier, neighbours)
+        pl.when(has_after)(x_copy.start)
+
+    core = space % 2
+    pl.when(core == 1)(send_plane)
     for d in range(4):
         split_rows(x_in[d], rows_f32.at[d], rows_bf, rows_sh, d + 1)
     w_par[:, :, :, 128:] = jnp.zeros((2, 9, WIN, 128), BF16)
@@ -170,6 +183,7 @@
             total1 = term1 if total1 is None else total1 + term1
         pre0[par] = total0
         pre1.append(total1)
+    pl.when(core == 0)(send_plane)
     loads[2].wait()
     acts = []
     for par in range(2):
@@ -178,20 +192,15 @@
         g1[par] = g
     side_by_side(acts[0], acts[1], act1)
     loads[3].wait()
-    turned = turn(perm, g1)
-    for tap in range(9):
-        part1[:, WIN * tap : WIN * tap + WIN] = dot(
-            turned, aligned_windows(rows_sh, tap // 3 + 2, tap % 3)
-        )
     pl.when(has_after)(x_copy.wait_send)
     pl.when(has_before)(x_copy.wait_recv)
 
 
 def second_kernel(
-    x_halo, cot_in, perm, rows_sh_in, w_par, pre0, g1, part1,
-    act0, grad, wg,
+    x_halo, cot_in, perm, rows_sh_in, w_par, pre0, g1,
+    act0, grad, gathered,
     rows_f32, rows_bf, rows_sh, g0, g2, part, part_bf, core_in,
-    own, chunks, chunk_in, summed, z_out, z_in, gathered, dx,
+    own, chunks, chunk_in, summed, z_out, z_in, dx,
     halo_send, halo_recv, core_send, core_recv,
     xy_send, xy_recv, z_send, z_recv, ag_send, ag_recv,
 ):
@@ -237,15 +246,9 @@
         value, g = pointwise(total, cotangent_rows(cot_in, 0, par))
         acts.append(value)
         g0[par] = g
-    turned = turn(perm, g0)
+    turned = jnp.concatenate([turn(perm, g0), turn(perm, g1)], axis=1)
 
     quarter = lax.broadcasted_iota(jnp.int32, (COUT, 128), 1) // 32
-
-    def full_tile(tap):
-        return 9 * (tap // 4) + 2 * (tap % 4)
-
-    def shared_tile(tap):
-        return 20 if tap == 8 else 9 * (tap // 4) + 8
 
     def place(tile, value):
         for half in range(2):
@@ -262,11 +265,8 @@
     shared = None
     for tap in range(9):
         a, b = tap // 3, tap % 3
-        if a == 0:
-            field = aligned_windows(rows_sh, 0, b)
-        else:
-            field = aligned_windows(rows_sh_in, a, b)
-        total = part1[:, WIN * tap : WIN * tap + WIN] + dot(turned, field)
+        low = aligned_windows(rows_sh, 0, b) if a == 0 else aligned_windows(rows_sh_in, a, b)
+        total = dot(turned, jnp.concatenate([low, aligned_windows(rows_sh_in, a + 2, b)], axis=0))
         place(full_tile(tap), total[:, 0:128])
         place(full_tile(tap) + 1, total[:, 128:256])
         rest = total[:, 256:384]
@@ -385,12 +385,13 @@
     for k, copy in zip(far_depth, z_copies):
         copy.wait()
         total = total + z_in[k - 1]
-    gathered[sample] = total * (1.0 / PEERS)
+    mine = pl.ds(pl.multiple_of(16 * sample, 16), 16)
+    gathered[mine] = total * (1.0 / PEERS)
 
     ag_copies = []
     for k in far_first:
         copy = pltpu.make_async_remote_copy(
-            src_ref=gathered.at[sample], dst_ref=gathered.at[sample],
+            src_ref=gathered.at[mine], dst_ref=gathered.at[mine],
             send_sem=ag_send.at[k - 1], recv_sem=ag_recv.at[k - 1],
             device_id={"sample": plane(k)}, device_id_type=MESH,
         )
@@ -398,10 +399,18 @@
         ag_copies.append(copy)
     for copy in ag_copies:
         copy.wait()
-    rows = gathered[...].reshape(16 * PEERS, 128)
+
+
+def hand_over(act0, act1, grad, gathered, act_hbm, grad_hbm, wg_hbm, wg, sems):
+    pairs = ((act0, act_hbm.at[0]), (act1, act_hbm.at[1]), (grad, grad_hbm), (wg, wg_hbm))
+    copies = [
+        pltpu.make_async_copy(src, dst, sems.at[n]) for n, (src, dst) in enumerate(pairs)
+    ]
+    for copy in copies[:3]:
+        copy.start()
 
     def tile_rows(tile):
-        return rows[MINE * tile : MINE * tile + MINE]
+        return gathered[MINE * tile : MINE * tile + MINE]
 
     for tap in range(9):
         rest = tile_rows(shared_tile(tap))[:, 32 * (tap % 4) : 32 * (tap % 4) + 32]
@@ -409,15 +418,7 @@
         window = jnp.concatenate([tile_rows(first), tile_rows(first + 1), rest], axis=1)
         for e in range(3):
             wg[3 * tap + e] = window[:, 96 * e : 96 * e + 96]
-
-
-def hand_over(act0, act1, grad, wg, act_hbm, grad_hbm, wg_hbm, sems):
-    pairs = ((act0, act_hbm.at[0]), (act1, act_hbm.at[1]), (grad, grad_hbm), (wg, wg_hbm))
-    copies = [
-        pltpu.make_async_copy(src, dst, sems.at[n]) for n, (src, dst) in enumerate(pairs)
-    ]
-    for copy in copies:
-        copy.start()
+    copies[3].start()
     for copy in copies:
         copy.wait()
 
@@ -457,11 +458,10 @@
             pltpu.VMEM((2, 9, WIN, 256), BF16),
             pltpu.VMEM((2, 128, 256), F32),
             pltpu.VMEM((2, 128, 256), BF16),
-            pltpu.VMEM((COUT, 9 * WIN), F32),
             pltpu.VMEM((16, LANES), BF16),
         ),
         in_specs=[in_hbm] * 4,
-        out_specs=(on_chip,) * 9,
+        out_specs=(on_chip,) * 8,
         scratch_shapes=[
             pltpu.VMEM((4, 32, LANES), BF16),
             pltpu.VMEM((9, 288, COUT), BF16),
@@ -474,14 +474,14 @@
         ),
         name="first_kernel",
     )(*(pltpu.with_memory_space_constraint(array, pltpu.HBM) for array in arguments))
-    act0, grad, wg = pl.pallas_call(
+    act0, grad, gathered = pl.pallas_call(
         second_kernel,
         out_shape=(
             pltpu.VMEM((16, LANES), BF16),
             pltpu.VMEM((4, 32, LANES), BF16),
-            pltpu.VMEM((27, MINE, 96), F32),
+            pltpu.VMEM((16 * PEERS, 128), F32),
         ),
-        in_specs=[on_chip] * 8,
+        in_specs=[on_chip] * 7,
         out_specs=(on_chip,) * 3,
         scratch_shapes=[
             pltpu.VMEM((24, 40, 128), F32),
@@ -498,7 +498,6 @@
             pltpu.VMEM((128, 128), F32),
             pltpu.VMEM((NZ, 16, 128), F32),
             pltpu.VMEM((NZ - 1, 16, 128), F32),
-            pltpu.VMEM((PEERS, 16, 128), F32),
             pltpu.VMEM((4, 24, 32, 128), F32),
             dma, dma, dma((PEERS,)), dma((PEERS,)),
             dma((PEERS - 1,)), dma((PEERS - 1,)), dma((NZ - 1,)), dma((NZ - 1,)),
@@ -518,10 +517,10 @@
         ),
         in_specs=[on_chip] * 4,
         out_specs=(any_space,) * 3,
-        scratch_shapes=[dma((4,))],
+        scratch_shapes=[pltpu.VMEM((27, MINE, 96), F32), dma((4,))],
         compiler_params=pltpu.CompilerParams(vmem_limit_bytes=4 << 20),
         name="hand_over",
-    )(*(held(array) for array in (act0, act1, grad, wg)))
+    )(*(held(array) for array in (act0, act1, grad, gathered)))
     return (
         activation.reshape(1, 2, 16, LANES),
         input_grad.reshape(1, 4, 32, LANES),

time: 37.8 us -> 37.6 us (level)
  no operation moved by 1% of the time
where the time goes in v5:
time: 37.6 us; the launch traced here: 37.5 us
  Pallas kernels  36.9 us (98%)
  between operations  0.65 us (2%)
    pallas_call x1, Pallas kernels, per_device(): pl.pallas_call(second_kernel, out_shape=(pltpu.VMEM((16, LANES), BF16), p...  31 us
    pallas_call x1, Pallas kernels, per_device(): pl.pallas_call(first_kernel, out_shape=(pltpu.VMEM((32, LANES), BF16), pl...  4.8 us
    pallas_call x1, Pallas kernels, per_device(): pl.pallas_call(hand_over, out_shape=(jax.ShapeDtypeStruct((2, 16, LANES),...  1.03 us

profile of v5, /device:TPU:2, one launch (start us, length us, event | category | flops | bytes accessed | tf_op | source)
XLA Modules:
  0.0 37.5 jit_solution(18162089697118062765)
XLA Ops:
  0.6 4.8 %first_kernel.1 = (bf16[32,3072]{1,0:T(8,128)(2,1)S(1)}, bf16[2,16,3072]{2,1,0:T(8,128)(2,1)S(1)}, bf16[192,256]{1,0:T(8,128)(2,1)S(1)}, bf16[2,3,5,16,3200]{4,3...) custom-call(bf16[4,32,3072]{2,1,0:T(8,128)(2,1)} %bitcast.9, ...), custom_call_target="tpu_custom_call" | custom-call | tf_op jit(solution)/shard_map/first_kernel/pallas_call | solution.py:451
  5.4 31.0 %second_kernel.1 = (bf16[16,3072]{1,0:T(8,128)(2,1)S(1)}, bf16[4,32,3072]{2,1,0:T(8,128)(2,1)S(1)}, f32[256,128]{1,0:T(8,128)S(1)}) custom-call(bf16[32,3072]{1,0:T(8,128)(2,1)S(1)} %get-tuple-element.17.x_halo, bf16[2,16,3072]{2,1,0:T(8,128)(2,1)S(1)} %get-tuple-element.18.cot_in, bf16[192,256]{1,0:T(8,128)(2,1)S(1)} %get-tuple-element.19.perm, ...), custom_call_target="tpu_custom_call" | custom-call | tf_op jit(solution)/shard_map/second_kernel/pallas_call | solution.py:477
  36.5 1.0 %hand_over.1 = (bf16[2,16,3072]{2,1,0:T(8,128)(2,1)}, bf16[4,32,3072]{2,1,0:T(8,128)(2,1)}, f32[27,12,96]{2,1,0:T(8,128)}) custom-call(bf16[16,3072]{1,0:T(8,128)(2,1)S(1)} %get-tuple-element.24.act0, bf16[16,3072]{1,0:T(8,128)(2,1)S(1)} %get-tuple-element.25.act1, bf16[4,32,3072]{2,1,0:T(8,128)(2,1)S(1)} %get-tuple-element.26.grad, ...), custom_call_target="tpu_custom_call" | custom-call | tf_op jit(solution)/shard_map/hand_over/pallas_call | solution.py:511

commit v6 on v5

--- a/solution.py
+++ b/solution.py
@@ -361,13 +361,13 @@
                         dx[2 * i + depth_par, 3 * m + u, pl.ds(row_par, 16, stride=2), :] = piece
     for d in range(4):
         for t in range(24):
-            grad[d, :, 128 * t : 128 * t + 128] = dx[d, t].astype(BF16)
+            grad[d, :, 128 * t : 128 * t + 128] = dx[d, t, 0:32].astype(BF16)
 
     total = own[...]
     for k, copy in zip(order, xy_copies):
         copy.wait()
         total = total + chunk_in[k - 1].astype(F32)
-    summed[...] = total.reshape(16 * UNITS, 128)
+    summed[0:128] = total.reshape(16 * UNITS, 128)
     for k in range(NZ):
         for t in range(2):
             z_out[k, pl.ds(t, 8, stride=2), :] = summed[pl.ds(2 * k + t, 8, stride=16), :]
@@ -375,13 +375,13 @@
     z_copies = []
     for k in far_depth:
         copy = pltpu.make_async_remote_copy(
-            src_ref=z_out.at[(z + k) % NZ], dst_ref=z_in.at[k - 1],
+            src_ref=z_out.at[(z + k) % NZ, 0:16], dst_ref=z_in.at[k - 1],
             send_sem=z_send.at[k - 1], recv_sem=z_recv.at[k - 1],
             device_id=depth(k), device_id_type=MESH,
         )
         copy.start()
         z_copies.append(copy)
-    total = z_out[z]
+    total = z_out[z, 0:16]
     for k, copy in zip(far_depth, z_copies):
         copy.wait()
         total = total + z_in[k - 1]
@@ -465,7 +465,7 @@
         scratch_shapes=[
             pltpu.VMEM((4, 32, LANES), BF16),
             pltpu.VMEM((9, 288, COUT), BF16),
-            pltpu.VMEM((4, 24, 40, 128), F32),
+            pltpu.VMEM((4, 24, 48, 128), F32),
             pltpu.VMEM((3, 5, 16, LANES + 128), BF16),
             dma((4,)), dma, dma,
         ],
@@ -484,7 +484,7 @@
         in_specs=[on_chip] * 7,
         out_specs=(on_chip,) * 3,
         scratch_shapes=[
-            pltpu.VMEM((24, 40, 128), F32),
+            pltpu.VMEM((24, 48, 128), F32),
             pltpu.VMEM((3, 1, 16, LANES + 128), BF16),
             pltpu.VMEM((2, 3, 1, 16, LANES + 128), BF16),
             pltpu.VMEM((2, 128, 256), BF16),
@@ -495,10 +495,10 @@
             pltpu.VMEM((UNITS, 16, 128), F32),
             pltpu.VMEM((PEERS - 1, UNITS, 16, 128), BF16),
             pltpu.VMEM((PEERS - 1, UNITS, 16, 128), BF16),
-            pltpu.VMEM((128, 128), F32),
-            pltpu.VMEM((NZ, 16, 128), F32),
+            pltpu.VMEM((144, 128), F32),
+            pltpu.VMEM((NZ, 24, 128), F32),
             pltpu.VMEM((NZ - 1, 16, 128), F32),
-            pltpu.VMEM((4, 24, 32, 128), F32),
+            pltpu.VMEM((4, 24, 40, 128), F32),
             dma, dma, dma((PEERS,)), dma((PEERS,)),
             dma((PEERS - 1,)), dma((PEERS - 1,)), dma((NZ - 1,)), dma((NZ - 1,)),
             dma((PEERS - 1,)), dma((PEERS - 1,)),

time: 37.6 us -> 37.6 us (level)
  no operation moved by 1% of the time
where the time goes in v6:
time: 37.6 us; the launch traced here: 37.5 us
  Pallas kernels  36.9 us (98%)
  between operations  0.65 us (2%)
    pallas_call x1, Pallas kernels, per_device(): pl.pallas_call(second_kernel, out_shape=(pltpu.VMEM((16, LANES), BF16), p...  31.1 us
    pallas_call x1, Pallas kernels, per_device(): pl.pallas_call(first_kernel, out_shape=(pltpu.VMEM((32, LANES), BF16), pl...  4.8 us
    pallas_call x1, Pallas kernels, per_device(): pl.pallas_call(hand_over, out_shape=(jax.ShapeDtypeStruct((2, 16, LANES),...  1.03 us

profile of v6, /device:TPU:2, one launch (start us, length us, event | category | flops | bytes accessed | tf_op | source)
XLA Modules:
  0.0 37.5 jit_solution(14844013842996143521)
XLA Ops:
  0.6 4.8 %first_kernel.1 = (bf16[32,3072]{1,0:T(8,128)(2,1)S(1)}, bf16[2,16,3072]{2,1,0:T(8,128)(2,1)S(1)}, bf16[192,256]{1,0:T(8,128)(2,1)S(1)}, bf16[2,3,5,16,3200]{4,3...) custom-call(bf16[4,32,3072]{2,1,0:T(8,128)(2,1)} %bitcast.9, ...), custom_call_target="tpu_custom_call" | custom-call | tf_op jit(solution)/shard_map/first_kernel/pallas_call | solution.py:451
  5.4 31.1 %second_kernel.1 = (bf16[16,3072]{1,0:T(8,128)(2,1)S(1)}, bf16[4,32,3072]{2,1,0:T(8,128)(2,1)S(1)}, f32[256,128]{1,0:T(8,128)S(1)}) custom-call(bf16[32,3072]{1,0:T(8,128)(2,1)S(1)} %get-tuple-element.17.x_halo, bf16[2,16,3072]{2,1,0:T(8,128)(2,1)S(1)} %get-tuple-element.18.cot_in, bf16[192,256]{1,0:T(8,128)(2,1)S(1)} %get-tuple-element.19.perm, ...), custom_call_target="tpu_custom_call" | custom-call | tf_op jit(solution)/shard_map/second_kernel/pallas_call | solution.py:477
  36.5 1.0 %hand_over.1 = (bf16[2,16,3072]{2,1,0:T(8,128)(2,1)}, bf16[4,32,3072]{2,1,0:T(8,128)(2,1)}, f32[27,12,96]{2,1,0:T(8,128)}) custom-call(bf16[16,3072]{1,0:T(8,128)(2,1)S(1)} %get-tuple-element.24.act0, bf16[16,3072]{1,0:T(8,128)(2,1)S(1)} %get-tuple-element.25.act1, bf16[4,32,3072]{2,1,0:T(8,128)(2,1)S(1)} %get-tuple-element.26.grad, ...), custom_call_target="tpu_custom_call" | custom-call | tf_op jit(solution)/shard_map/hand_over/pallas_call | solution.py:511

commit v7 on v6

--- a/solution.py
+++ b/solution.py
@@ -214,6 +214,11 @@
     def plane(k):
         return ((y + k // NX) % NY) * NX + (x + k % NX) % NX
 
+    def mirrored(k, side):
+        dy, dx_ = k // NX, k % NX
+        dy, dx_ = dy + side * (NY - 2 * dy), dx_ + side * (NX - 2 * dx_)
+        return ((y + dy) % NY) * NX + (x + dx_) % NX
+
     def depth(k):
         return {"space": ((z + k) % NZ) * 2 + core}
 
@@ -284,7 +289,7 @@
     order = far_first + [0]
     core_copies = []
     for k in order:
-        c = plane(k)
+        c = mirrored(k, 1 - core)
         copy = pltpu.make_async_remote_copy(
             src_ref=part_bf.at[1 - core, units(c)], dst_ref=core_in.at[units(c)],
             send_sem=core_send.at[k], recv_sem=core_recv.at[k],
@@ -295,7 +300,7 @@
     xy_copies = []
     for k, copy in zip(order, core_copies):
         copy.wait()
-        c = plane(k)
+        c = mirrored(k, core)
         total = part[core, units(c)] + core_in[units(c)].astype(F32)
         if k == 0:
             own[...] = total

time: 37.6 us -> 37.6 us (level)
  no operation moved by 1% of the time
where the time goes in v7:
time: 37.6 us; the launch traced here: 37.5 us
  Pallas kernels  36.9 us (98%)
  between operations  0.65 us (2%)
    pallas_call x1, Pallas kernels, per_device(): pl.pallas_call(second_kernel, out_shape=(pltpu.VMEM((16, LANES), BF16), p...  31.1 us
    pallas_call x1, Pallas kernels, per_device(): pl.pallas_call(first_kernel, out_shape=(pltpu.VMEM((32, LANES), BF16), pl...  4.8 us
    pallas_call x1, Pallas kernels, per_device(): pl.pallas_call(hand_over, out_shape=(jax.ShapeDtypeStruct((2, 16, LANES),...  1.03 us

profile of v7, /device:TPU:2, one launch (start us, length us, event | category | flops | bytes accessed | tf_op | source)
XLA Modules:
  0.0 37.5 jit_solution(13103314722094246714)
XLA Ops:
  0.6 4.8 %first_kernel.1 = (bf16[32,3072]{1,0:T(8,128)(2,1)S(1)}, bf16[2,16,3072]{2,1,0:T(8,128)(2,1)S(1)}, bf16[192,256]{1,0:T(8,128)(2,1)S(1)}, bf16[2,3,5,16,3200]{4,3...) custom-call(bf16[4,32,3072]{2,1,0:T(8,128)(2,1)} %bitcast.9, ...), custom_call_target="tpu_custom_call" | custom-call | tf_op jit(solution)/shard_map/first_kernel/pallas_call | solution.py:456
  5.4 31.1 %second_kernel.1 = (bf16[16,3072]{1,0:T(8,128)(2,1)S(1)}, bf16[4,32,3072]{2,1,0:T(8,128)(2,1)S(1)}, f32[256,128]{1,0:T(8,128)S(1)}) custom-call(bf16[32,3072]{1,0:T(8,128)(2,1)S(1)} %get-tuple-element.17.x_halo, bf16[2,16,3072]{2,1,0:T(8,128)(2,1)S(1)} %get-tuple-element.18.cot_in, bf16[192,256]{1,0:T(8,128)(2,1)S(1)} %get-tuple-element.19.perm, ...), custom_call_target="tpu_custom_call" | custom-call | tf_op jit(solution)/shard_map/second_kernel/pallas_call | solution.py:482
  36.5 1.0 %hand_over.1 = (bf16[2,16,3072]{2,1,0:T(8,128)(2,1)}, bf16[4,32,3072]{2,1,0:T(8,128)(2,1)}, f32[27,12,96]{2,1,0:T(8,128)}) custom-call(bf16[16,3072]{1,0:T(8,128)(2,1)S(1)} %get-tuple-element.24.act0, bf16[16,3072]{1,0:T(8,128)(2,1)S(1)} %get-tuple-element.25.act1, bf16[4,32,3072]{2,1,0:T(8,128)(2,1)S(1)} %get-tuple-element.26.grad, ...), custom_call_target="tpu_custom_call" | custom-call | tf_op jit(solution)/shard_map/hand_over/pallas_call | solution.py:516

commit v8 on v7

--- a/solution.py
+++ b/solution.py
@@ -398,7 +398,7 @@
         copy = pltpu.make_async_remote_copy(
             src_ref=gathered.at[mine], dst_ref=gathered.at[mine],
             send_sem=ag_send.at[k - 1], recv_sem=ag_recv.at[k - 1],
-            device_id={"sample": plane(k)}, device_id_type=MESH,
+            device_id={"sample": mirrored(k, core)}, device_id_type=MESH,
         )
         copy.start()
         ag_copies.append(copy)

time: 37.6 us -> 37.6 us (level)
  no operation moved by 1% of the time
where the time goes in v8:
time: 37.6 us; the launch traced here: 37.5 us
  Pallas kernels  36.9 us (98%)
  between operations  0.65 us (2%)
    pallas_call x1, Pallas kernels, per_device(): pl.pallas_call(second_kernel, out_shape=(pltpu.VMEM((16, LANES), BF16), p...  31.1 us
    pallas_call x1, Pallas kernels, per_device(): pl.pallas_call(first_kernel, out_shape=(pltpu.VMEM((32, LANES), BF16), pl...  4.8 us
    pallas_call x1, Pallas kernels, per_device(): pl.pallas_call(hand_over, out_shape=(jax.ShapeDtypeStruct((2, 16, LANES),...  1.03 us

profile of v8, /device:TPU:2, one launch (start us, length us, event | category | flops | bytes accessed | tf_op | source)
XLA Modules:
  0.0 37.5 jit_solution(16927817369967909479)
XLA Ops:
  0.6 4.8 %first_kernel.1 = (bf16[32,3072]{1,0:T(8,128)(2,1)S(1)}, bf16[2,16,3072]{2,1,0:T(8,128)(2,1)S(1)}, bf16[192,256]{1,0:T(8,128)(2,1)S(1)}, bf16[2,3,5,16,3200]{4,3...) custom-call(bf16[4,32,3072]{2,1,0:T(8,128)(2,1)} %bitcast.9, ...), custom_call_target="tpu_custom_call" | custom-call | tf_op jit(solution)/shard_map/first_kernel/pallas_call | solution.py:456
  5.4 31.1 %second_kernel.1 = (bf16[16,3072]{1,0:T(8,128)(2,1)S(1)}, bf16[4,32,3072]{2,1,0:T(8,128)(2,1)S(1)}, f32[256,128]{1,0:T(8,128)S(1)}) custom-call(bf16[32,3072]{1,0:T(8,128)(2,1)S(1)} %get-tuple-element.17.x_halo, bf16[2,16,3072]{2,1,0:T(8,128)(2,1)S(1)} %get-tuple-element.18.cot_in, bf16[192,256]{1,0:T(8,128)(2,1)S(1)} %get-tuple-element.19.perm, ...), custom_call_target="tpu_custom_call" | custom-call | tf_op jit(solution)/shard_map/second_kernel/pallas_call | solution.py:482
  36.5 1.0 %hand_over.1 = (bf16[2,16,3072]{2,1,0:T(8,128)(2,1)}, bf16[4,32,3072]{2,1,0:T(8,128)(2,1)}, f32[27,12,96]{2,1,0:T(8,128)}) custom-call(bf16[16,3072]{1,0:T(8,128)(2,1)S(1)} %get-tuple-element.24.act0, bf16[16,3072]{1,0:T(8,128)(2,1)S(1)} %get-tuple-element.25.act1, bf16[4,32,3072]{2,1,0:T(8,128)(2,1)S(1)} %get-tuple-element.26.grad, ...), custom_call_target="tpu_custom_call" | custom-call | tf_op jit(solution)/shard_map/hand_over/pallas_call | solution.py:516
